TPU v7x, 32 devices: a whole 2x2x4 slice. The times are simulated.
32 devices in a mesh: seq: 8 (over z, y), mp: 4 (over x, core).
Axes of the slice: x: 2, y: 2, z: 4, core: 2. Of those that a mesh axis runs over, the one named last changes fastest.
Arguments:
- queries: bfloat16 [4096, 8192], P('seq', 'mp'), may hold values from -6 to 6
- keys_in: bfloat16 [4096, 8192], P('seq', 'mp'), may hold values from -6 to 6
- values_in: bfloat16 [4096, 8192], P('seq', 'mp'), may hold values from -6 to 6
- residual: bfloat16 [4096, 8192], P('seq', 'mp')
- short_taps: bfloat16 [3, 7, 8192], P(None, None, 'mp'), may hold values from -2 to 2
- mr_filter: bfloat16 [128, 512], P('seq', 'mp'), may hold values from -0.5 to 0.5
- norm_gain: bfloat16 [8192], P('mp'), may hold values from 0.5 to 1.5
- predecessor: int32 [8], replicated, may hold values from -1 to 7, as said below
- stretch_lengths: int32 [8], replicated, may hold values from 1 to 512, as said below
Outputs:
- mixed: bfloat16 [4096, 8192], P('seq', 'mp')
- normed: bfloat16 [4096, 8192], P('seq', 'mp')
Inputs may be any that keep to these rules, and one draw needn't show every extreme that they name: predecessor[j] is the stretch holding the preceding 512 tokens of stretch j's genome, or -1 for a genome's first stretch; each stretch precedes at most one stretch, and the chains have no cycles. `stretch_lengths`: every stretch that precedes another stretch is full (512 valid tokens); valid tokens come first.
All inputs are finite; a program needn't handle non-finite values.
Results may differ from a plain program's by a relative error of at most 0.0049.
Values may be sent and summed in bfloat16 or wider, within the bound.
No kernel may reach another device: no remote copies, remote signals or barrier semaphores. Data moves between devices by JAX's collectives and lax.ppermute only.
A program may use at most 64 MiB of HBM per device.

v0:
```python
import jax
import jax.numpy as jnp
from jax import lax
from jax.sharding import PartitionSpec as P

EPSILON = 1e-06


def featurize(extended, taps):
    length = extended.shape[0] - 8
    total = jnp.zeros((length, extended.shape[1]), jnp.float32)
    for offset in range(taps.shape[0]):
        total = total + taps[offset].astype(jnp.float32) * extended[
            8 - offset : 8 - offset + length
        ].astype(jnp.float32)
    return total


def toeplitz_blocks(filter_rows):
    tap_count = filter_rows.shape[0]
    group_count = filter_rows.shape[1]
    flipped = filter_rows[::-1].T
    pattern = jnp.concatenate(
        [
            jnp.zeros((group_count, 1), filter_rows.dtype),
            flipped,
            jnp.zeros((group_count, tap_count), filter_rows.dtype),
        ],
        axis=1,
    )
    tiled = jnp.tile(pattern, (1, tap_count))[:, : 2 * tap_count * tap_count]
    return tiled.reshape(group_count, tap_count, 2 * tap_count)


def long_conv(extended, filter_rows, group_size):
    tap_count = filter_rows.shape[0]
    length = extended.shape[0] - tap_count
    blocks = length // tap_count
    channels = extended.shape[1]
    pieces = extended.reshape(blocks + 1, tap_count, channels)
    windows = jnp.concatenate([pieces[:-1], pieces[1:]], axis=1).reshape(
        blocks, 2 * tap_count, channels // group_size, group_size
    )
    matrices = toeplitz_blocks(filter_rows)
    result = jnp.einsum("gij,bjgc->bigc", matrices, windows, preferred_element_type=jnp.float32)
    return result.reshape(length, channels)


def body(
    queries,
    keys_in,
    values_in,
    residual,
    short_taps,
    mr_filter,
    norm_gain,
    predecessor,
    stretch_lengths,
):
    row_count, width = queries.shape
    device = lax.axis_index("seq")
    filter_rows = lax.all_gather(mr_filter, "seq", axis=0, tiled=True)
    tap_count = filter_rows.shape[0]
    group_size = width // filter_rows.shape[1]
    blank = jnp.zeros((8, width), queries.dtype)
    key_feat = featurize(jnp.concatenate([blank, keys_in]), short_taps[1])
    value_feat = featurize(jnp.concatenate([blank, values_in]), short_taps[2])
    mixed_in = (key_feat * value_feat).astype(jnp.bfloat16)
    state_tail = mixed_in[row_count - tap_count :][None]
    raw_tail = jnp.concatenate(
        [queries[row_count - 8 :], keys_in[row_count - 8 :], values_in[row_count - 8 :]], axis=1
    )[None]
    source = predecessor[device]
    carry = (jnp.zeros_like(state_tail), jnp.zeros_like(raw_tail))
    piece = (
        lax.all_gather(state_tail, "seq", axis=0, tiled=True),
        lax.all_gather(raw_tail, "seq", axis=0, tiled=True),
    )
    count = piece[0].shape[0]
    inside = (source >= 0) & (source < count)
    offset = jnp.clip(source, 0, count - 1)
    prev_state, prev_raw = tuple(
        (
            jnp.where(inside, lax.dynamic_slice_in_dim(member, offset, 1, 0), kept)
            for member, kept in zip(piece, carry)
        )
    )
    prev_rows = prev_raw[0]
    prev_query = prev_rows[:, :width]
    prev_key = prev_rows[:, width : 2 * width]
    prev_value = prev_rows[:, 2 * width :]
    query_feat = featurize(jnp.concatenate([prev_query, queries]), short_taps[0])
    head_key = featurize(jnp.concatenate([prev_key, keys_in[:8]]), short_taps[1])
    head_value = featurize(jnp.concatenate([prev_value, values_in[:8]]), short_taps[2])
    head_mixed = (head_key * head_value).astype(jnp.bfloat16)
    mixed_in = jnp.concatenate([head_mixed, mixed_in[8:]])
    extended = jnp.concatenate([prev_state[0], mixed_in])
    filtered = long_conv(extended, filter_rows, group_size)
    valid = (jnp.arange(row_count, dtype=jnp.int32) < stretch_lengths[device])[:, None]
    mixed = jnp.where(valid, query_feat * filtered, 0.0).astype(jnp.bfloat16)
    summed = residual.astype(jnp.float32) + mixed.astype(jnp.float32)
    squares_total = lax.psum(jnp.sum(summed * summed, axis=1), "mp")
    scale_rows = lax.rsqrt(squares_total / (width * lax.axis_size("mp")) + EPSILON)
    normed = jnp.where(
        valid, summed * scale_rows[:, None] * norm_gain.astype(jnp.float32), 0.0
    ).astype(jnp.bfloat16)
    return (mixed, normed)


def solution(mesh):
    in_specs = (
        P("seq", "mp"),
        P("seq", "mp"),
        P("seq", "mp"),
        P("seq", "mp"),
        P(None, None, "mp"),
        P("seq", "mp"),
        P("mp"),
        P(),
        P(),
    )
    out_specs = (P("seq", "mp"), P("seq", "mp"))
    return jax.shard_map(body, mesh=mesh, in_specs=in_specs, out_specs=out_specs, check_vma=False)
```

profile of v0, /device:TPU:0, one launch (start us, length us, event | category | flops | bytes accessed | tf_op | source)
XLA Modules:
  0.0 210.2 jit_solution(4456971975261556778)
XLA Ops:
  8.1 1.5 slice_convert_fusion.20
  9.5 16.2 %multiply_convert_fusion = bf16[512,2048]{1,0:T(8,128)(2,1)S(1)} fusion(bf16[512,2048]{1,0:T(8,128)(2,1)} %param.11, bf16[512,2048]{1,0:T(8,128)(2,1)} %param.10, f32[2048]{0:T(1024)S(1)} %bitcast.85, f32[2048]{0:T(1024)S(1)} %bitcast.83, f32[2048]{0:T(1024)S(1)} %bitcast.59, f32[2048]{0:T(1024)S(1)} %bitcast.61, f32[2048]{0:T(1024)S(1)} %bitcast.63, ...), kind=kLoop, calls=%fused_computation.15 | loop fusion | flops 44040192 | bytes 6406144 | tf_op jit(solution)/shard_map/convert_element_type | solution.py:68
  29.9 3.9 %copy.54 = bf16[512,2048]{0,1:T(8,128)(2,1)} copy(bf16[512,2048]{1,0:T(8,128)(2,1)} %param.9) | data formatting | bytes 4194304 | tf_op args[0]
  33.9 2.9 %copy.63 = bf16[512,2048]{0,1:T(8,128)(2,1)S(1)} copy(bf16[512,2048]{1,0:T(8,128)(2,1)} %param.12) | data formatting | bytes 4194304 | tf_op args[3]
  36.8 32.6 %all_gather.11 = bf16[128,128]{1,0:T(8,128)(2,1)S(1)} all-gather(bf16[16,128]{1,0:T(8,128)(2,1)S(1)} %copy-done.2), channel_id=1, replica_groups=mesh['seq'=8,'mp'=4] {'seq'}, dimensions={0}, use_global_device_ids=true | all-gather | bytes 36864 | tf_op jit(solution)/shard_map/all_gather | solution.py:62
  69.6 4.5 %tile.4 = bf16[128,128,257]{0,2,1:T(8,128)(2,1)} broadcast(bf16[128,257]{0,1:T(8,128)(2,1)S(1)} %maximum_maximum_fusion), dimensions={0,2} | broadcast | bytes 8487168 | tf_op jit(solution)/shard_map/tile | solution.py:31
  74.1 12.9 %tile.10 = bf16[128,32896]{0,1:T(8,128)(2,1)} reshape(bf16[128,128,257]{0,2,1:T(8,128)(2,1)} %tile.4) | data formatting | bytes 16842752 | tf_op jit(solution)/shard_map/tile | solution.py:31
  87.0 7.1 %slice.352 = bf16[128,32768]{0,1:T(8,128)(2,1)} slice(bf16[128,32896]{0,1:T(8,128)(2,1)} %tile.10), slice={[0:128], [0:32768]} | slice | bytes 16777216 | tf_op jit(solution)/shard_map/slice | solution.py:31
  94.1 13.0 %copy.66 = bf16[128,128,256,1]{2,1,3,0:T(8,128)(2,1)} copy(bf16[128,128,256,1]{0,2,1,3:T(8,128)(2,1)} %bitcast.55) | data formatting | bytes 16777216 | tf_op jit(solution)/shard_map/reshape | solution.py:32
  108.5 31.9 %all-gather = bf16[64,6144]{1,0:T(8,128)(2,1)S(1)} all-gather(bf16[8,6144]{1,0:T(8,128)(2,1)S(1)} %pad_maximum_fusion.4), channel_id=2, replica_groups=mesh['seq'=8,'mp'=4] {'seq'}, dimensions={0}, use_global_device_ids=true | all-gather | bytes 884736 | tf_op jit(solution)/shard_map/all_gather | solution.py:77
  143.3 3.7 %pad_maximum_fusion = (bf16[512,2048]{1,0:T(8,128)(2,1)}, bf16[512,2048]{1,0:T(8,128)(2,1)}) fusion(bf16[504,2048]{1,0:T(8,128)(2,1)} %slice.351, bf16[8,2048]{1,0:T(8,128)(2,1)S(1)} %multiply_convert_fusion.1, bf16[128,2048]{1,0:T(8,128)(2,1)S(1)} %select_bitcast_fusion), kind=kLoop, calls=%fused_computation.27 | loop fusion | flops 10485760 | bytes 6815744 | tf_op jit(solution)/shard_map/concatenate | solution.py:97
  147.0 3.9 %copy.58 = bf16[512,2048]{0,1:T(8,128)(2,1)} copy(bf16[512,2048]{1,0:T(8,128)(2,1)} %get-tuple-element.9) | data formatting | bytes 4194304 | tf_op jit(solution)/shard_map/concatenate | solution.py:97
  151.0 4.0 %concatenate.44 = bf16[4,128,128,16]{1,0,3,2:T(4,128)(2,1)} reshape(bf16[512,2048]{0,1:T(8,128)(2,1)} %copy.58) | data formatting | bytes 4194304 | tf_op jit(solution)/shard_map/concatenate | solution.py:41
  154.9 3.5 %copy.60 = bf16[4,128,128,16]{1,3,0,2:T(8,128)(2,1)} copy(bf16[4,128,128,16]{1,0,3,2:T(4,128)(2,1)} %concatenate.44) | data formatting | bytes 4194304 | tf_op jit(solution)/shard_map/concatenate | solution.py:41
  158.4 3.9 %copy.57 = bf16[512,2048]{0,1:T(8,128)(2,1)} copy(bf16[512,2048]{1,0:T(8,128)(2,1)} %get-tuple-element.8) | data formatting | bytes 4194304 | tf_op jit(solution)/shard_map/slice | solution.py:41
  162.3 4.0 %concatenate.42 = bf16[4,128,128,16]{1,0,3,2:T(4,128)(2,1)} reshape(bf16[512,2048]{0,1:T(8,128)(2,1)} %copy.57) | data formatting | bytes 4194304 | tf_op jit(solution)/shard_map/concatenate | solution.py:41
  166.3 2.3 %copy.59 = bf16[4,128,128,16]{1,3,0,2:T(8,128)(2,1)S(1)} copy(bf16[4,128,128,16]{1,0,3,2:T(4,128)(2,1)} %concatenate.42) | data formatting | bytes 4194304 | tf_op jit(solution)/shard_map/concatenate | solution.py:41
  168.6 6.4 %fusion.6 = f32[4,128,128,16]{1,3,0,2:T(8,128)S(1)} fusion(bf16[128,128,256,1]{2,1,3,0:T(8,128)(2,1)} %copy.66, bf16[4,128,128,16]{1,3,0,2:T(8,128)(2,1)S(1)} %copy-done.1, bf16[4,128,128,16]{1,3,0,2:T(8,128)(2,1)S(1)} %copy.59), kind=kOutput, calls=%fused_computation.21 | convolution fusion | flops 545259520 | bytes 16777216 | tf_op jit(solution)/shard_map/gij,bjgc->bigc/dot_general | solution.py:45
  175.0 2.1 copy.62
  177.1 8.9 %multiply_reduce_fusion = (f32[512]{0:T(512)S(1)}, bf16[512,2048]{0,1:T(8,128)(2,1)}) fusion(bf16[512,2048]{0,1:T(8,128)(2,1)S(1)} %copy.63, f32[256,8,4,128]{3,2,1,0:T(4,128)S(1)} %bitcast.56, bf16[512,2048]{0,1:T(8,128)(2,1)S(1)} %copy-done, bf16[8,2048]{0,1:T(8,128)(2,1)S(1)} %copy.55, f32[2048]{0:T(1024)S(1)} %bitcast.89, f32[2048]{0:T(1024)S(1)} %bitcast.90, ...), kind=kLoop, calls=%fused_computation.13 | loop fusion | flops 48233984 | bytes 10578432 | tf_op jit(solution)/shard_map/reduce_sum | solution.py:102
  186.1 3.9 %copy.64 = bf16[512,2048]{1,0:T(8,128)(2,1)} copy(bf16[512,2048]{0,1:T(8,128)(2,1)} %get-tuple-element.7) | data formatting | bytes 4194304
  190.0 5.6 %psum.7 = f32[512]{0:T(512)S(1)} all-reduce(f32[512]{0:T(512)S(1)} %get-tuple-element.6), channel_id=1, replica_groups=mesh['seq'=8,'mp'=4] {'mp'}, use_global_device_ids=true, to_apply=%region_1.2 | all-reduce | flops 512 | bytes 4096 | tf_op jit(solution)/shard_map/psum | solution.py:102
  195.6 3.8 %select_convert_fusion = bf16[512,2048]{0,1:T(8,128)(2,1)} fusion(bf16[512,2048]{0,1:T(8,128)(2,1)} %get-tuple-element.7, bf16[512,2048]{0,1:T(8,128)(2,1)S(1)} %copy.63, f32[2048]{0:T(1024)S(1)} %convert_element_type.432, f32[512]{0:T(512)S(1)} %add_rsqrt_fusion, pred[512]{0:T(512)(128)(4,1)S(1)} %iota_compare_fusion), kind=kLoop, calls=%fused_computation.12 | loop fusion | flops 7340032 | bytes 6302208 | tf_op jit(solution)/shard_map/convert_element_type | solution.py:106
  199.4 3.9 %copy.65 = bf16[512,2048]{1,0:T(8,128)(2,1)} copy(bf16[512,2048]{0,1:T(8,128)(2,1)} %select_convert_fusion) | data formatting | bytes 4194304
  (37 shorter events, 7.8 us)
Async XLA Ops:
  7.2 135.1 %all-gather.4.cloned.1.call-start = ((), (), s32[]{:S(2)}) async-start(), calls=%async_computation | async-start | bytes 4718592 | tf_op jit(solution)/shard_map/all_gather | solution.py:76
  25.7 2.3 %copy-start.4 = (s32[8]{0:T(128)S(1)}, s32[8]{0:T(128)}, u32[]{:S(2)}) copy-start(s32[8]{0:T(128)} %param.16) | copy-start | bytes 100
  29.9 6.8 %copy-start.2 = (bf16[16,128]{1,0:T(8,128)(2,1)S(1)}, bf16[16,128]{1,0:T(8,128)(2,1)}, u32[]{:S(2)}) copy-start(bf16[16,128]{1,0:T(8,128)(2,1)} %param.14) | copy-start | bytes 12292
  94.1 14.5 %slice-start = ((bf16[512,2048]{1,0:T(8,128)(2,1)}), bf16[8,2048]{1,0:T(8,128)(2,1)S(1)}, s32[]{:S(2)}) async-start(bf16[512,2048]{1,0:T(8,128)(2,1)} %param.9), calls=%async_computation.1 | async-start | bytes 65536 | tf_op jit(solution)/shard_map/slice | solution.py:71
  94.1 46.7 %copy-start.5 = (s32[8]{0:T(128)S(1)}, s32[8]{0:T(128)}, u32[]{:S(2)}) copy-start(s32[8]{0:T(128)} %param.17) | copy-start | bytes 100
  94.1 47.3 %copy-start.3 = (bf16[2048]{0:T(1024)(128)(2,1)S(1)}, bf16[2048]{0:T(1024)(128)(2,1)}, u32[]{:S(2)}) copy-start(bf16[2048]{0:T(1024)(128)(2,1)} %param.15) | copy-start | bytes 12292
  166.3 2.3 %copy-start.1 = (bf16[4,128,128,16]{1,3,0,2:T(8,128)(2,1)S(1)}, bf16[4,128,128,16]{1,3,0,2:T(8,128)(2,1)}, u32[]{:S(2)}) copy-start(bf16[4,128,128,16]{1,3,0,2:T(8,128)(2,1)} %copy.60) | copy-start | bytes 6291460
  175.0 2.1 copy-start
Sparse Core Ops, SparseCore 0:
  26.7 76.2 all-gather.3
where the time goes:
time: 212 us; the launch traced here: 210 us
  local copies, waits for them, and re-layouts  80.4 us (38%)
  blocking collectives  70.1 us (33%)
  other arithmetic  37.1 us (18%)
  between operations  16.2 us (8%)
  matrix products  6.39 us (3%)
    all_gather x1, blocking collectives, body(): filter_rows = lax.all_gather(mr_filter, 'seq', axis=0, tiled=True)  32.6 us
    all_gather x1, blocking collectives, body(): lax.all_gather(raw_tail, 'seq', axis=0, tiled=True)  31.9 us
    another operation x2, local copies, waits for them, and re-layouts, toeplitz_blocks(): tiled = jnp.tile(pattern, (1, tap_count))[:, :2 * tap_count * tap_count]  17.4 us
    convert_element_type x1, other arithmetic, body(): mixed_in = (key_feat * value_feat).astype(jnp.bfloat16)  16.2 us
    unnamed x16, local copies, waits for them, and re-layouts  14.6 us
    concatenate x4, local copies, waits for them, and re-layouts, long_conv(): jnp.concatenate([pieces[:-1], pieces[1:]], axis=1)  13.8 us
    reshape x1, local copies, waits for them, and re-layouts, toeplitz_blocks(): return tiled.reshape(group_count, tap_count, 2 * tap_count)  13 us
    reduce_sum x1, other arithmetic, body(): squares_total = lax.psum(jnp.sum(summed * summed, axis=1), 'mp')  8.94 us
  transfers between devices with their start and end apart: 1, of which 0 were waited for; matrix products, arithmetic and copies ran while one was open for 23% of the time, Pallas kernels for 0%

commit v1 on v0

v1 whole, which is shorter than its diff:
```python
import functools

import jax
import jax.numpy as jnp
from jax import lax
from jax.experimental import pallas as pl
from jax.experimental.pallas import tpu as pltpu
from jax.sharding import PartitionSpec as P

EPSILON = 1e-06
F32 = jnp.float32
BF16 = jnp.bfloat16
LANES = 128
STEP = 256
BLOCK = 64
WINDOW = 256
PACKED = 160
OPENING = 144
VMEM_LIMIT = 48 * 1024 * 1024


def params():
    return pltpu.CompilerParams(vmem_limit_bytes=VMEM_LIMIT)


def cost(flops, bytes_accessed):
    return pl.CostEstimate(flops=flops, bytes_accessed=bytes_accessed, transcendentals=0)


def short_conv(scratch, taps, start, rows):
    total = None
    for offset in range(taps.shape[0]):
        term = taps[offset : offset + 1] * scratch[pl.ds(start + 8 - offset, rows), :]
        total = term if total is None else total + term
    return total


def tail_kernel(width_taps, q_ref, k_ref, v_ref, kb_ref, vb_ref, taps_ref, filt_ref, out_ref, ks, vs):
    taps = taps_ref[...].astype(F32)
    pieces = []
    for lane in range(0, STEP, LANES):
        cols = slice(lane, lane + LANES)
        ks[0:16, :] = kb_ref[:, cols].astype(F32)
        vs[0:16, :] = vb_ref[:, cols].astype(F32)
        ks[16:144, :] = k_ref[:, cols].astype(F32)
        vs[16:144, :] = v_ref[:, cols].astype(F32)
        for row in range(0, 128, 64):
            key = short_conv(ks, taps[1, :, cols], row + 8, 64)
            value = short_conv(vs, taps[2, :, cols], row + 8, 64)
            out_ref[0, row : row + 64, cols] = (key * value).astype(BF16)
        last = [q_ref[:, cols].astype(F32)[8:], ks[136:144, :], vs[136:144, :]]
        if filt_ref is None:
            last.append(jnp.zeros((8, LANES), F32))
        else:
            first = lane // LANES * 8
            last.append(filt_ref[...].astype(F32)[first : first + 8])
        pieces.append(jnp.concatenate(last))
    out_ref[0, 128:160, :] = jnp.concatenate(pieces, axis=1).astype(BF16)


def tail_call(queries, keys_in, values_in, short_taps, mr_filter):
    rows, width = queries.shape
    steps = width // STEP
    packed = mr_filter is not None
    in_specs = [
        pl.BlockSpec((16, STEP), lambda p: (rows // 16 - 1, p)),
        pl.BlockSpec((128, STEP), lambda p: (rows // 128 - 1, p)),
        pl.BlockSpec((128, STEP), lambda p: (rows // 128 - 1, p)),
        pl.BlockSpec((16, STEP), lambda p: (rows // 16 - 9, p)),
        pl.BlockSpec((16, STEP), lambda p: (rows // 16 - 9, p)),
        pl.BlockSpec((3, 7, STEP), lambda p: (0, 0, p)),
    ]
    operands = [queries, keys_in, values_in, keys_in, values_in, short_taps]
    body = functools.partial(tail_kernel, 7)
    if packed:
        in_specs.append(pl.BlockSpec((16, LANES), lambda p: (0, 0)))
        operands.append(mr_filter)
    else:
        body = lambda *refs: tail_kernel(7, *refs[:6], None, *refs[6:])
    return pl.pallas_call(
        body,
        grid=(steps,),
        in_specs=in_specs,
        out_specs=pl.BlockSpec((1, PACKED, STEP), lambda p: (p, 0, 0)),
        out_shape=jax.ShapeDtypeStruct((steps, PACKED, STEP), BF16),
        scratch_shapes=[pltpu.VMEM((144, LANES), F32), pltpu.VMEM((144, LANES), F32)],
        compiler_params=params(),
        cost_estimate=cost(128 * width * 30, 128 * width * 6),
        name="tail",
    )(*operands)


def feature_kernel(k_ref, v_ref, taps_ref, out_ref, ks, vs):
    rows = k_ref.shape[0]
    taps = taps_ref[...].astype(F32)
    for lane in range(0, STEP, LANES):
        cols = slice(lane, lane + LANES)
        ks[0:8, :] = jnp.zeros((8, LANES), F32)
        vs[0:8, :] = jnp.zeros((8, LANES), F32)
        ks[8 : rows + 8, :] = k_ref[:, cols].astype(F32)
        vs[8 : rows + 8, :] = v_ref[:, cols].astype(F32)
        for row in range(0, rows, 64):
            key = short_conv(ks, taps[1, :, cols], row, 64)
            value = short_conv(vs, taps[2, :, cols], row, 64)
            out_ref[row : row + 64, cols] = (key * value).astype(BF16)


def feature_call(keys_in, values_in, short_taps):
    rows, width = keys_in.shape
    block = pl.BlockSpec((rows, STEP), lambda p: (0, p))
    return pl.pallas_call(
        feature_kernel,
        grid=(width // STEP,),
        in_specs=[block, block, pl.BlockSpec((3, 7, STEP), lambda p: (0, 0, p))],
        out_specs=block,
        out_shape=jax.ShapeDtypeStruct((rows, width), BF16),
        scratch_shapes=[pltpu.VMEM((rows + 8, LANES), F32), pltpu.VMEM((rows + 8, LANES), F32)],
        compiler_params=params(),
        cost_estimate=cost(rows * width * 30, rows * width * 6),
        name="features",
    )(keys_in, values_in, short_taps)


def route_kernel(pred_ref, in_ref, out_ref, filt_ref):
    for j in range(in_ref.shape[0]):
        out_ref[j] = in_ref[jnp.maximum(pred_ref[j], 0)]
        last = in_ref[j, 144:160, :].astype(F32)[8:]
        filt_ref[16 * j : 16 * j + 16, :] = jnp.concatenate([last[:, :LANES], last[:, LANES:]]).astype(BF16)


def route_call(predecessor, received):
    count = received.shape[0]
    return pl.pallas_call(
        route_kernel,
        in_specs=[pl.BlockSpec(memory_space=pltpu.SMEM), pl.BlockSpec(memory_space=pltpu.VMEM)],
        out_specs=[pl.BlockSpec(memory_space=pltpu.VMEM)] * 2,
        out_shape=[
            jax.ShapeDtypeStruct(received.shape, BF16),
            jax.ShapeDtypeStruct((16 * count, LANES), BF16),
        ],
        compiler_params=params(),
        name="route",
    )(predecessor, received)


def pick_groups(result, group_size, rows=BLOCK):
    shape = (rows, result.shape[1])
    group = (lax.broadcasted_iota(jnp.int32, shape, 1) & (LANES - 1)) // group_size
    picked = result[:rows]
    for g in range(1, LANES // group_size):
        picked = jnp.where(group == g, result[g * rows : (g + 1) * rows], picked)
    return picked


def main_kernel(group_size, len_ref, q_ref, u_ref, res_ref, taps_ref, filt_ref, mixed_ref, toep_ref, sum_ref, qs, spread, acc):
    step = pl.program_id(0)
    rows = q_ref.shape[0]
    per_lane = LANES // group_size
    per_step = STEP // group_size
    length = len_ref[lax.axis_index("seq")]

    @pl.when(step == 0)
    def _():
        tap_count = filt_ref.shape[0]
        tap = lax.broadcasted_iota(jnp.int32, (tap_count, WINDOW), 0)
        place = lax.broadcasted_iota(jnp.int32, (tap_count, WINDOW), 1)
        onehot = (place == WINDOW - BLOCK - tap).astype(BF16)
        spread[...] = lax.dot_general(
            filt_ref[...], onehot, (((0,), (0,)), ((), ())), preferred_element_type=F32
        )
        acc[...] = jnp.zeros_like(acc)

    taps = taps_ref[...].astype(F32)
    mixed_ref[0:128, :] = jnp.zeros((128, STEP), BF16)
    base = pl.multiple_of(step * per_step, per_step)
    line_block = spread[pl.ds(base, per_step), :]
    for g in range(per_step):
        line = jnp.broadcast_to(line_block[g : g + 1], (BLOCK, WINDOW))
        toep_ref[g * BLOCK : (g + 1) * BLOCK, :] = pltpu.roll(line, 0, 1, stride=1, stride_axis=0).astype(BF16)
    for tile in range(STEP // LANES):
        cols = slice(tile * LANES, (tile + 1) * LANES)
        qs[0:8, :] = jnp.zeros((8, LANES), F32)
        qs[8 : rows + 8, :] = q_ref[:, cols].astype(F32)
        matrix = toep_ref[tile * per_lane * BLOCK : (tile + 1) * per_lane * BLOCK, :]
        for start in range(128, rows, 2 * BLOCK):
            windows = []
            for first in (start, start + BLOCK):
                low = first + BLOCK - WINDOW
                if low < 0:
                    windows.append(
                        jnp.concatenate([jnp.zeros((-low, LANES), BF16), u_ref[0 : first + BLOCK, cols]])
                    )
                else:
                    windows.append(u_ref[low : first + BLOCK, cols])
            result = jnp.dot(matrix, jnp.concatenate(windows, axis=1), preferred_element_type=F32)
            picked = pick_groups(result, group_size)
            for half in range(2):
                first = start + half * BLOCK
                filtered = picked[:, half * LANES : (half + 1) * LANES]
                query = short_conv(qs, taps[0, :, cols], first, BLOCK)
                row = lax.broadcasted_iota(jnp.int32, (BLOCK, LANES), 0) + first
                mixed = jnp.where(row < length, query * filtered, 0.0).astype(BF16)
                mixed_ref[first : first + BLOCK, cols] = mixed
                summed = res_ref[first : first + BLOCK, cols].astype(F32) + mixed.astype(F32)
                acc[first - 128 : first - 128 + BLOCK, :] += summed * summed

    @pl.when(step == pl.num_programs(0) - 1)
    def _():
        sum_ref[...] = jnp.sum(acc[...].T, axis=0, keepdims=True)


def main_call(group_size, stretch_lengths, queries, mixed_in, residual, short_taps, filter_rows):
    rows, width = queries.shape
    per_step = STEP // group_size
    groups = filter_rows.shape[1]
    block = pl.BlockSpec((rows, STEP), lambda p, *_: (0, p))
    return pl.pallas_call(
        functools.partial(main_kernel, group_size),
        grid_spec=pltpu.PrefetchScalarGridSpec(
            num_scalar_prefetch=1,
            grid=(width // STEP,),
            in_specs=[
                block,
                block,
                block,
                pl.BlockSpec((3, 7, STEP), lambda p, *_: (0, 0, p)),
                pl.BlockSpec(filter_rows.shape, lambda p, *_: (0, 0)),
            ],
            out_specs=[
                block,
                pl.BlockSpec((per_step * BLOCK, WINDOW), lambda p, *_: (p, 0)),
                pl.BlockSpec((1, rows - 128), lambda p, *_: (0, 0)),
            ],
            scratch_shapes=[
                pltpu.VMEM((rows + 8, LANES), F32),
                pltpu.VMEM((groups, WINDOW), F32),
                pltpu.VMEM((rows - 128, LANES), F32),
            ],
        ),
        out_shape=[
            jax.ShapeDtypeStruct((rows, width), BF16),
            jax.ShapeDtypeStruct((groups * BLOCK, WINDOW), BF16),
            jax.ShapeDtypeStruct((1, rows - 128), F32),
        ],
        compiler_params=params(),
        cost_estimate=cost(rows * width * 2 * WINDOW * 8, rows * width * 12),
        name="conv",
    )(stretch_lengths, queries, mixed_in, residual, short_taps, filter_rows)


def head_kernel(group_size, pred_ref, len_ref, prev_ref, q_ref, k_ref, v_ref, u_ref, res_ref, taps_ref, toep_ref, part_ref, kept_ref, mixed_ref, sum_ref, qs, ks, vs, acc):
    del kept_ref
    step = pl.program_id(0)
    per_lane = LANES // group_size
    device = lax.axis_index("seq")
    length = len_ref[device]
    follows = pred_ref[device] >= 0

    @pl.when(step == 0)
    def _():
        acc[...] = jnp.zeros_like(acc)

    taps = taps_ref[...].astype(F32)
    for tile in range(STEP // LANES):
        cols = slice(tile * LANES, (tile + 1) * LANES)
        prev = jnp.where(follows, prev_ref[0, 128:160, cols].astype(F32), 0.0)
        qs[0:8, :] = prev[0:8]
        ks[0:8, :] = prev[8:16]
        vs[0:8, :] = prev[16:24]
        qs[8 : OPENING + 8, :] = q_ref[:, cols].astype(F32)
        ks[8:24, :] = k_ref[:, cols].astype(F32)
        vs[8:24, :] = v_ref[:, cols].astype(F32)
        key = short_conv(ks, taps[1, :, cols], 0, 16)
        value = short_conv(vs, taps[2, :, cols], 0, 16)
        opening = (key * value).astype(BF16)
        state = prev_ref[0, 0:128, cols]
        state = jnp.where(follows, state, jnp.zeros_like(state))
        extended = jnp.concatenate([jnp.zeros((64, LANES), BF16), state, opening, u_ref[16:192, cols]])
        windows = jnp.concatenate([extended[0:WINDOW], extended[BLOCK : BLOCK + WINDOW]], axis=1)
        matrix = toep_ref[tile * per_lane * BLOCK : (tile + 1) * per_lane * BLOCK, :]
        result = jnp.dot(matrix, windows, preferred_element_type=F32)
        picked = pick_groups(result, group_size)
        edge = OPENING - 2 * BLOCK
        edge_matrix = jnp.concatenate([matrix[g * BLOCK : g * BLOCK + edge] for g in range(per_lane)])
        edge_result = jnp.dot(edge_matrix, extended[2 * BLOCK : 2 * BLOCK + WINDOW], preferred_element_type=F32)
        parts = [
            (0, BLOCK, picked[:, :LANES]),
            (BLOCK, BLOCK, picked[:, LANES:]),
            (2 * BLOCK, edge, pick_groups(edge_result, group_size, edge)),
        ]
        for first, rows, filtered in parts:
            query = short_conv(qs, taps[0, :, cols], first, rows)
            row = lax.broadcasted_iota(jnp.int32, (rows, LANES), 0) + first
            mixed = jnp.where(row < length, query * filtered, 0.0).astype(BF16)
            mixed_ref[first : first + rows, cols] = mixed
            summed = res_ref[first : first + rows, cols].astype(F32) + mixed.astype(F32)
            acc[first : first + rows, :] += summed * summed

    @pl.when(step == pl.num_programs(0) - 1)
    def _():
        opening_sum = jnp.sum(acc[...].T, axis=0, keepdims=True)
        lane = lax.broadcasted_iota(jnp.int32, (1, LANES), 1)
        edge_sum = jnp.where(lane < OPENING - LANES, opening_sum[:, LANES:], part_ref[:, :LANES])
        sum_ref[...] = jnp.concatenate([opening_sum[:, :LANES], edge_sum, part_ref[:, LANES:]], axis=1)


def head_call(group_size, predecessor, stretch_lengths, previous, queries, keys_in, values_in, mixed_in, residual, short_taps, toeplitz, partial_sum, mixed):
    rows, width = queries.shape
    per_step = STEP // group_size
    block = pl.BlockSpec((OPENING, STEP), lambda p, *_: (0, p))
    small = pl.BlockSpec((16, STEP), lambda p, *_: (0, p))
    return pl.pallas_call(
        functools.partial(head_kernel, group_size),
        grid_spec=pltpu.PrefetchScalarGridSpec(
            num_scalar_prefetch=2,
            grid=(width // STEP,),
            in_specs=[
                pl.BlockSpec((1, PACKED, STEP), lambda p, *_: (p, 0, 0)),
                block,
                small,
                small,
                pl.BlockSpec((192, STEP), lambda p, *_: (0, p)),
                block,
                pl.BlockSpec((3, 7, STEP), lambda p, *_: (0, 0, p)),
                pl.BlockSpec((per_step * BLOCK, WINDOW), lambda p, *_: (p, 0)),
                pl.BlockSpec(partial_sum.shape, lambda p, *_: (0, 0)),
                pl.BlockSpec(memory_space=pl.ANY),
            ],
            out_specs=[block, pl.BlockSpec((1, rows), lambda p, *_: (0, 0))],
            scratch_shapes=[
                pltpu.VMEM((OPENING + 8, LANES), F32),
                pltpu.VMEM((24, LANES), F32),
                pltpu.VMEM((24, LANES), F32),
                pltpu.VMEM((256, LANES), F32),
            ],
        ),
        out_shape=[
            jax.ShapeDtypeStruct((rows, width), BF16),
            jax.ShapeDtypeStruct((1, rows), F32),
        ],
        input_output_aliases={11: 0},
        compiler_params=params(),
        cost_estimate=cost(128 * width * 2 * WINDOW * 8, 128 * width * 12),
        name="head",
    )(predecessor, stretch_lengths, previous, queries, keys_in, values_in, mixed_in, residual, short_taps, toeplitz, partial_sum, mixed)


def norm_kernel(channels, rows, len_ref, sum_ref, mixed_ref, res_ref, gain_ref, out_ref):
    first = pl.program_id(0) * rows
    length = len_ref[lax.axis_index("seq")]
    scale_line = lax.rsqrt(sum_ref[...] / channels + EPSILON)
    scale = jnp.broadcast_to(scale_line, (LANES, rows)).T
    row = lax.broadcasted_iota(jnp.int32, (rows, LANES), 0) + first
    scale = jnp.where(row < length, scale, 0.0)
    valid = row < length
    for lane in range(0, mixed_ref.shape[1], LANES):
        cols = slice(lane, lane + LANES)
        gain = gain_ref[:, cols].astype(F32)
        summed = res_ref[:, cols].astype(F32) + mixed_ref[:, cols].astype(F32)
        out_ref[:, cols] = jnp.where(valid, summed * scale * gain, 0.0).astype(BF16)


def norm_call(channels, stretch_lengths, total, mixed, residual, norm_gain):
    rows, width = mixed.shape
    block = pl.BlockSpec((128, width), lambda p, *_: (p, 0))
    return pl.pallas_call(
        functools.partial(norm_kernel, channels, 128),
        grid_spec=pltpu.PrefetchScalarGridSpec(
            num_scalar_prefetch=1,
            grid=(rows // 128,),
            in_specs=[
                pl.BlockSpec((1, 128), lambda p, *_: (0, p)),
                block,
                block,
                pl.BlockSpec((1, width), lambda p, *_: (0, 0)),
            ],
            out_specs=block,
        ),
        out_shape=jax.ShapeDtypeStruct((rows, width), BF16),
        compiler_params=params(),
        cost_estimate=cost(rows * width * 6, rows * width * 6),
        name="norm",
    )(stretch_lengths, total, mixed, residual, norm_gain.reshape(1, width))


def exchange(pieces):
    return lax.all_to_all(pieces, "seq", split_axis=0, concat_axis=0, tiled=True)


def body(queries, keys_in, values_in, residual, short_taps, mr_filter, norm_gain, predecessor, stretch_lengths):
    rows, width = queries.shape
    count = lax.axis_size("seq")
    parts = lax.axis_size("mp")
    group_size = width // mr_filter.shape[1]
    two_phase = width // STEP == count and mr_filter.shape == (16, LANES)
    if two_phase:
        packed = tail_call(queries, keys_in, values_in, short_taps, mr_filter)
        received = exchange(packed)
        mixed_in = feature_call(keys_in, values_in, short_taps)
        routed, filter_rows = route_call(predecessor, received)
        previous = exchange(routed)
    else:
        packed = tail_call(queries, keys_in, values_in, short_taps, None)
        gathered = lax.all_gather(packed[None], "seq", axis=0, tiled=True)
        source = jnp.clip(predecessor[lax.axis_index("seq")], 0, count - 1)
        previous = lax.dynamic_index_in_dim(gathered, source, 0, keepdims=False)
        filter_rows = lax.all_gather(mr_filter, "seq", axis=0, tiled=True)
        mixed_in = feature_call(keys_in, values_in, short_taps)
    mixed, toeplitz, partial_sum = main_call(
        group_size, stretch_lengths, queries, mixed_in, residual, short_taps, filter_rows
    )
    mixed, squares = head_call(
        group_size, predecessor, stretch_lengths, previous, queries, keys_in, values_in, mixed_in,
        residual, short_taps, toeplitz, partial_sum, mixed,
    )
    total = lax.psum(squares, "mp")
    normed = norm_call(width * parts, stretch_lengths, total, mixed, residual, norm_gain)
    return (mixed, normed)


def solution(mesh):
    in_specs = (
        P("seq", "mp"),
        P("seq", "mp"),
        P("seq", "mp"),
        P("seq", "mp"),
        P(None, None, "mp"),
        P("seq", "mp"),
        P("mp"),
        P(),
        P(),
    )
    out_specs = (P("seq", "mp"), P("seq", "mp"))
    return jax.shard_map(body, mesh=mesh, in_specs=in_specs, out_specs=out_specs, check_vma=False)
```

time: 212 us -> 82.1 us (0.39)
  local copies, waits for them, and re-layouts: 80.4 us -> 10.9 us
  blocking collectives: 70.1 us -> 30.7 us
  other arithmetic: 37.1 us -> 0 us
  Pallas kernels: 0 us -> 35.1 us
  between operations: 16.2 us -> 0.76 us
  matrix products: 6.39 us -> 0 us
  starting transfers between devices: 0.04 us -> 3.54 us
    all_gather x2 -> x0, blocking collectives: 64.4 us -> none  [the longest x1 32.6 us: body(): filter_rows = lax.all_gather(mr_filter, 'seq', axis=0, tiled=True)]
    pallas_call x0 -> x6, Pallas kernels: none -> 35.1 us  [the longest x1 10.8 us: main_call(): pl.pallas_call(functools.partial(main_kernel, group_size), grid_spec=pltp...]
    all_to_all x0 -> x1, blocking collectives: none -> 24.9 us  [exchange(): lax.all_to_all(pieces, 'seq', split_axis=0, concat_axis=0, tiled=True)]
    convert_element_type x6 -> x0, other arithmetic: 22.5 us -> none  [the longest x1 16.2 us: body(): mixed_in = (key_feat * value_feat).astype(jnp.bfloat16)]
    concatenate x7 -> x0, local copies, waits for them, and re-layouts: 17.8 us -> none  [the longest x4 13.8 us: long_conv(): jnp.concatenate([pieces[:-1], pieces[1:]], axis=1)]
    another operation x2 -> x0, local copies, waits for them, and re-layouts: 17.4 us -> none  [toeplitz_blocks(): tiled = jnp.tile(pattern, (1, tap_count))[:, :2 * tap_count * tap_count]]
    slice x9 -> x0, local copies, waits for them, and re-layouts: 14.4 us -> none  [the longest x1 7.08 us: toeplitz_blocks(): tiled = jnp.tile(pattern, (1, tap_count))[:, :2 * tap_count * tap_count]]
    reshape x1, local copies, waits for them, and re-layouts: 13 us -> 0.01 us  [norm_call(): norm_gain.reshape(1, width)]
  transfers between devices with their start and end apart: 1 -> 1, of which waited for: 0 -> 0; matrix products, arithmetic and copies ran while one was open for 23% -> 0% of each run, Pallas kernels for 0% -> 22%
where the time goes in v1:
time: 82.1 us; the launch traced here: 81 us
  Pallas kernels  35.1 us (43%)
  blocking collectives  30.7 us (37%)
  local copies, waits for them, and re-layouts  10.9 us (13%)
  starting transfers between devices  3.54 us (4%)
    all_to_all x1, blocking collectives, exchange(): lax.all_to_all(pieces, 'seq', split_axis=0, concat_axis=0, tiled=True)  24.9 us
    unnamed x28, local copies, waits for them, and re-layouts  10.9 us
    pallas_call x1, Pallas kernels, main_call(): pl.pallas_call(functools.partial(main_kernel, group_size), grid_spec=pltp...  10.8 us
    pallas_call x1, Pallas kernels, head_call(): pl.pallas_call(functools.partial(head_kernel, group_size), grid_spec=pltp...  8.3 us
    pallas_call x1, Pallas kernels, feature_call(): pl.pallas_call(feature_kernel, grid=(width // STEP,), in_specs=[block, bl...  7.08 us
    psum x1, blocking collectives, body(): total = lax.psum(squares, 'mp')  5.76 us
    pallas_call x1, Pallas kernels, tail_call(): pl.pallas_call(body, grid=(steps,), in_specs=in_specs, out_specs=pl.Block...  4.27 us
    all_to_all x1, starting transfers between devices, exchange(): lax.all_to_all(pieces, 'seq', split_axis=0, concat_axis=0, tiled=True)  3.54 us
  transfers between devices with their start and end apart: 1, of which 0 were waited for; matrix products, arithmetic and copies ran while one was open for 0% of the time, Pallas kernels for 22%

profile of v1, /device:TPU:0, one launch (start us, length us, event | category | flops | bytes accessed | tf_op | source)
XLA Modules:
  0.0 81.0 jit_solution(4511296581909511124)
XLA Ops:
  0.6 0.0 copy-start
  0.6 1.6 %copy-done = bf16[512,2048]{1,0:T(8,128)(2,1)S(1)} copy-done((bf16[512,2048]{1,0:T(8,128)(2,1)S(1)}, bf16[512,2048]{1,0:T(8,128)(2,1)}, u32[]{:S(2)}) %copy-start) | copy-done | bytes 2097176
  2.2 1.6 %copy-done.2 = bf16[512,2048]{1,0:T(8,128)(2,1)S(1)} copy-done((bf16[512,2048]{1,0:T(8,128)(2,1)S(1)}, bf16[512,2048]{1,0:T(8,128)(2,1)}, u32[]{:S(2)}) %copy-start.2) | copy-done | bytes 2097176
  3.8 0.9 %copy-done.8 = bf16[3,7,2048]{2,1,0:T(8,128)(2,1)S(1)} copy-done((bf16[3,7,2048]{2,1,0:T(8,128)(2,1)S(1)}, bf16[3,7,2048]{2,1,0:T(8,128)(2,1)}, u32[]{:S(2)}) %copy-start.8) | copy-done | bytes 86040
  4.7 0.7 copy-done.10
  5.4 4.3 %tail.1 = bf16[8,160,256]{2,1,0:T(8,128)(2,1)S(1)} custom-call(bf16[512,2048]{1,0:T(8,128)(2,1)S(1)} %copy-done.2, bf16[512,2048]{1,0:T(8,128)(2,1)S(1)} %copy-done, bf16[512,2048]{1,0:T(8,128)(2,1)} %v_ref.5, bf16[512,2048]{1,0:T(8,128)(2,1)S(1)} %copy-done, bf16[512,2048]{1,0:T(8,128)(2,1)} %v_ref.5, bf16[3,7,2048]{2,1,0:T(8,128)(2,1)S(1)} %copy-done.8, ...), custom_call_target="tpu_custom_call" | custom-call | flops 7864320 | bytes 1572864 | tf_op jit(solution)/shard_map/tail/pallas_call | solution.py:80
  9.7 0.0 copy-start.13
  9.7 0.0 copy-start.1
  9.7 0.0 copy-start.9
  9.7 24.9 %all_to_all.10.in_ref = bf16[8,160,256]{2,1,0:T(8,128)(2,1)S(1)} all-to-all(bf16[8,160,256]{2,1,0:T(8,128)(2,1)S(1)} %tail.1), channel_id=1, replica_groups=mesh['seq'=8,'mp'=4] {'seq'}, dimensions={0} | all-to-all | bytes 1310720 | tf_op jit(solution)/shard_map/all_to_all | solution.py:387
  34.6 1.4 %route.1 = (bf16[8,160,256]{2,1,0:T(8,128)(2,1)}, bf16[128,128]{1,0:T(8,128)(2,1)S(1)}) custom-call(s32[8]{0:T(128)S(1)} %copy-done.12, bf16[8,160,256]{2,1,0:T(8,128)(2,1)S(1)} %all_to_all.10.in_ref), custom_call_target="tpu_custom_call" | custom-call | tf_op jit(solution)/shard_map/route/pallas_call | solution.py:133
  36.1 3.5 %all-to-all-start.1 = ((bf16[8,160,256]{2,1,0:T(8,128)(2,1)}), bf16[8,160,256]{2,1,0:T(8,128)(2,1)S(1)}, u32[]{:S(2)}, u32[]{:S(2)}) async-start(bf16[8,160,256]{2,1,0:T(8,128)(2,1)} %get-tuple-element.9), calls=%async_computation.1 | async-start | bytes 1310720 | tf_op jit(solution)/shard_map/all_to_all | solution.py:387
  39.7 0.0 copy-start.3
  39.7 0.0 copy-start.11
  39.7 7.1 %features.1.u_ref = bf16[512,2048]{1,0:T(8,128)(2,1)S(1)} custom-call(bf16[512,2048]{1,0:T(8,128)(2,1)S(1)} %copy-done.1, bf16[512,2048]{1,0:T(8,128)(2,1)} %v_ref.5, bf16[3,7,2048]{2,1,0:T(8,128)(2,1)S(1)} %copy-done.9), custom_call_target="tpu_custom_call" | custom-call | flops 31457280 | bytes 6291456 | tf_op jit(solution)/shard_map/features/pallas_call | solution.py:111
  46.8 10.8 %conv.1 = (bf16[512,2048]{1,0:T(8,128)(2,1)}, bf16[8192,256]{1,0:T(8,128)(2,1)}, f32[1,384]{1,0:T(1,128)S(1)}) custom-call(s32[8]{0:T(128)S(1)} %copy-done.11, bf16[512,2048]{1,0:T(8,128)(2,1)S(1)} %copy-done.3, bf16[512,2048]{1,0:T(8,128)(2,1)S(1)} %features.1.u_ref, bf16[512,2048]{1,0:T(8,128)(2,1)} %res_ref.5, bf16[3,7,2048]{2,1,0:T(8,128)(2,1)S(1)} %copy-done.9, ...), custom_call_target="tpu_custom_call" | custom-call | flops 4294967296 | bytes 12582912 | tf_op jit(solution)/shard_map/conv/pallas_call | solution.py:217
  57.6 1.3 %copy-done.6 = bf16[512,2048]{1,0:T(8,128)(2,1)} copy-done((bf16[512,2048]{1,0:T(8,128)(2,1)}, bf16[512,2048]{1,0:T(8,128)(2,1)S(1)}, u32[]{:S(2)}) %copy-start.6) | copy-done | bytes 2097176
  58.9 0.0 all-to-all-done.1.prev_ref
  58.9 1.6 %copy-done.4 = bf16[512,2048]{1,0:T(8,128)(2,1)S(1)} copy-done((bf16[512,2048]{1,0:T(8,128)(2,1)S(1)}, bf16[512,2048]{1,0:T(8,128)(2,1)}, u32[]{:S(2)}) %copy-start.4) | copy-done | bytes 2097176
  60.5 8.3 %head.1 = (bf16[512,2048]{1,0:T(8,128)(2,1)}, f32[1,512]{1,0:T(1,128)S(1)}) custom-call(s32[8]{0:T(128)S(1)} %copy-done.12, s32[8]{0:T(128)S(1)} %copy-done.11, bf16[8,160,256]{2,1,0:T(8,128)(2,1)S(1)} %all-to-all-done.1.prev_ref, bf16[512,2048]{1,0:T(8,128)(2,1)S(1)} %copy-done.4, ...), custom_call_target="tpu_custom_call", output_to_operand_aliasing={{0}: (11, {})} | custom-call | flops 1073741824 | bytes 3145728 | tf_op jit(solution)/shard_map/head/pallas_call | solution.py:312
  68.8 5.8 %psum.7.sum_ref = f32[1,512]{1,0:T(1,128)S(1)} all-reduce(f32[1,512]{1,0:T(1,128)S(1)} %get-tuple-element.15), channel_id=1, replica_groups=mesh['seq'=8,'mp'=4] {'mp'}, use_global_device_ids=true, to_apply=%region_0.0 | all-reduce | flops 512 | bytes 4096 | tf_op jit(solution)/shard_map/psum | solution.py:416
  74.5 1.6 %copy-done.5 = bf16[512,2048]{1,0:T(8,128)(2,1)S(1)} copy-done((bf16[512,2048]{1,0:T(8,128)(2,1)S(1)}, bf16[512,2048]{1,0:T(8,128)(2,1)}, u32[]{:S(2)}) %copy-start.5) | copy-done | bytes 2097176
  76.1 1.6 %copy-done.7 = bf16[512,2048]{1,0:T(8,128)(2,1)S(1)} copy-done((bf16[512,2048]{1,0:T(8,128)(2,1)S(1)}, bf16[512,2048]{1,0:T(8,128)(2,1)}, u32[]{:S(2)}) %copy-start.7) | copy-done | bytes 2097176
  77.7 3.2 %norm.1 = bf16[512,2048]{1,0:T(8,128)(2,1)} custom-call(s32[8]{0:T(128)S(1)} %copy-done.11, f32[1,512]{1,0:T(1,128)S(1)} %psum.7.sum_ref, bf16[512,2048]{1,0:T(8,128)(2,1)S(1)} %copy-done.7, bf16[512,2048]{1,0:T(8,128)(2,1)S(1)} %copy-done.5, bf16[1,2048]{1,0:T(2,128)(2,1)S(1)} %reshape.7.gain_ref), custom_call_target="tpu_custom_call" | custom-call | flops 6291456 | bytes 6291456 | tf_op jit(solution)/shard_map/norm/pallas_call | solution.py:366
  (15 shorter events, 0.0 us)
Async XLA Ops:
  0.6 1.6 %copy-start = (bf16[512,2048]{1,0:T(8,128)(2,1)S(1)}, bf16[512,2048]{1,0:T(8,128)(2,1)}, u32[]{:S(2)}) copy-start(bf16[512,2048]{1,0:T(8,128)(2,1)} %k_ref.5) | copy-start | bytes 6291460
  2.2 1.6 %copy-start.2 = (bf16[512,2048]{1,0:T(8,128)(2,1)S(1)}, bf16[512,2048]{1,0:T(8,128)(2,1)}, u32[]{:S(2)}) copy-start(bf16[512,2048]{1,0:T(8,128)(2,1)} %q_ref.5) | copy-start | bytes 6291460
  3.8 0.9 %copy-start.8 = (bf16[3,7,2048]{2,1,0:T(8,128)(2,1)S(1)}, bf16[3,7,2048]{2,1,0:T(8,128)(2,1)}, u32[]{:S(2)}) copy-start(bf16[3,7,2048]{2,1,0:T(8,128)(2,1)} %taps_ref.7) | copy-start | bytes 258052
  4.7 0.7 copy-start.10
  5.4 29.2 %copy-start.12 = (s32[8]{0:T(128)S(1)}, s32[8]{0:T(128)}, u32[]{:S(2)}) copy-start(s32[8]{0:T(128)} %pred_ref.3) | copy-start | bytes 100
  9.7 29.9 %copy-start.13 = (bf16[2048]{0:T(1024)(128)(2,1)S(1)}, bf16[2048]{0:T(1024)(128)(2,1)}, u32[]{:S(2)}) copy-start(bf16[2048]{0:T(1024)(128)(2,1)} %param.15) | copy-start | bytes 12292
  9.7 30.0 %copy-start.1 = (bf16[512,2048]{1,0:T(8,128)(2,1)S(1)}, bf16[512,2048]{1,0:T(8,128)(2,1)}, u32[]{:S(2)}) copy-start(bf16[512,2048]{1,0:T(8,128)(2,1)} %k_ref.5) | copy-start | bytes 6291460
  9.7 30.0 %copy-start.9 = (bf16[3,7,2048]{2,1,0:T(8,128)(2,1)S(1)}, bf16[3,7,2048]{2,1,0:T(8,128)(2,1)}, u32[]{:S(2)}) copy-start(bf16[3,7,2048]{2,1,0:T(8,128)(2,1)} %taps_ref.7) | copy-start | bytes 258052
  36.1 22.8 %all-to-all-start.1 = ((bf16[8,160,256]{2,1,0:T(8,128)(2,1)}), bf16[8,160,256]{2,1,0:T(8,128)(2,1)S(1)}, u32[]{:S(2)}, u32[]{:S(2)}) async-start(bf16[8,160,256]{2,1,0:T(8,128)(2,1)} %get-tuple-element.9), calls=%async_computation.1 | async-start | bytes 1310720 | tf_op jit(solution)/shard_map/all_to_all | solution.py:387
  39.7 7.1 %copy-start.3 = (bf16[512,2048]{1,0:T(8,128)(2,1)S(1)}, bf16[512,2048]{1,0:T(8,128)(2,1)}, u32[]{:S(2)}) copy-start(bf16[512,2048]{1,0:T(8,128)(2,1)} %q_ref.5) | copy-start | bytes 6291460
  39.7 7.1 %copy-start.11 = (s32[8]{0:T(128)S(1)}, s32[8]{0:T(128)}, u32[]{:S(2)}) copy-start(s32[8]{0:T(128)} %len_ref.5) | copy-start | bytes 100
  57.6 1.3 %copy-start.6 = (bf16[512,2048]{1,0:T(8,128)(2,1)}, bf16[512,2048]{1,0:T(8,128)(2,1)S(1)}, u32[]{:S(2)}) copy-start(bf16[512,2048]{1,0:T(8,128)(2,1)S(1)} %features.1.u_ref) | copy-start | bytes 6291460
  58.9 1.6 %copy-start.4 = (bf16[512,2048]{1,0:T(8,128)(2,1)S(1)}, bf16[512,2048]{1,0:T(8,128)(2,1)}, u32[]{:S(2)}) copy-start(bf16[512,2048]{1,0:T(8,128)(2,1)} %q_ref.5) | copy-start | bytes 6291460
  74.5 1.6 %copy-start.5 = (bf16[512,2048]{1,0:T(8,128)(2,1)S(1)}, bf16[512,2048]{1,0:T(8,128)(2,1)}, u32[]{:S(2)}) copy-start(bf16[512,2048]{1,0:T(8,128)(2,1)} %res_ref.5) | copy-start | bytes 6291460
  76.1 1.6 %copy-start.7 = (bf16[512,2048]{1,0:T(8,128)(2,1)S(1)}, bf16[512,2048]{1,0:T(8,128)(2,1)}, u32[]{:S(2)}) copy-start(bf16[512,2048]{1,0:T(8,128)(2,1)} %get-tuple-element.7.mixed_ref) | copy-start | bytes 6291460

commit v2 on v1

v2 whole, which is shorter than its diff:
```python
import functools

import jax
import jax.numpy as jnp
from jax import lax
from jax.experimental import pallas as pl
from jax.experimental.pallas import tpu as pltpu
from jax.sharding import PartitionSpec as P

EPSILON = 1e-06
F32 = jnp.float32
BF16 = jnp.bfloat16
LANES = 128
STEP = 256
WIDE = 512
BLOCK = 64
WINDOW = 256
PACKED = 160
OPENING = 144
VMEM_LIMIT = 60 * 1024 * 1024


def params():
    return pltpu.CompilerParams(vmem_limit_bytes=VMEM_LIMIT)


def cost(flops, bytes_accessed):
    return pl.CostEstimate(flops=flops, bytes_accessed=bytes_accessed, transcendentals=0)


def short_conv(scratch, taps, start, rows):
    total = None
    for offset in range(taps.shape[0]):
        term = taps[offset : offset + 1] * scratch[pl.ds(start + 8 - offset, rows), :]
        total = term if total is None else total + term
    return total


def tail_kernel(slots, swapped, packed, q_ref, k_ref, v_ref, kb_ref, vb_ref, taps_ref, filt_ref, *rest):
    outs, (held, ks, vs) = rest[:slots], rest[slots:]
    device = lax.axis_index("seq")

    def piece(slot, carry):
        first = (jnp.bitwise_xor(slot, device) if swapped else slot) * STEP
        lasts = []
        for tile in range(STEP // LANES):
            cols = pl.ds(pl.multiple_of(first + tile * LANES, LANES), LANES)
            here = slice(tile * LANES, (tile + 1) * LANES)
            kt, vt = ks.at[tile], vs.at[tile]
            kt[0:16, :] = kb_ref[:, cols].astype(F32)
            vt[0:16, :] = vb_ref[:, cols].astype(F32)
            kt[16:144, :] = k_ref[:, cols].astype(F32)
            vt[16:144, :] = v_ref[:, cols].astype(F32)
            key_taps = taps_ref[1, :, cols].astype(F32)
            value_taps = taps_ref[2, :, cols].astype(F32)
            for row in range(0, 128, 64):
                key = short_conv(kt, key_taps, row + 8, 64)
                value = short_conv(vt, value_taps, row + 8, 64)
                held[slot, row : row + 64, here] = (key * value).astype(BF16)
            last = [q_ref[:, cols].astype(F32)[8:], kt[136:144, :], vt[136:144, :]]
            if packed:
                last.append(filt_ref[...].astype(F32)[8 * tile : 8 * tile + 8])
            else:
                last.append(jnp.zeros((8, LANES), F32))
            lasts.append(jnp.concatenate(last))
        held[slot, 128:PACKED, :] = jnp.concatenate(lasts, axis=1).astype(BF16)
        return carry

    lax.fori_loop(0, slots, piece, 0)
    for slot in range(slots):
        outs[slot][...] = held[slot]


def tail_call(swapped, packed, queries, keys_in, values_in, short_taps, mr_filter):
    rows, width = queries.shape
    slots = width // STEP
    return pl.pallas_call(
        functools.partial(tail_kernel, slots, swapped, packed),
        grid=(1,),
        in_specs=[
            pl.BlockSpec((16, width), lambda p: (rows // 16 - 1, 0)),
            pl.BlockSpec((128, width), lambda p: (rows // 128 - 1, 0)),
            pl.BlockSpec((128, width), lambda p: (rows // 128 - 1, 0)),
            pl.BlockSpec((16, width), lambda p: (rows // 16 - 9, 0)),
            pl.BlockSpec((16, width), lambda p: (rows // 16 - 9, 0)),
            pl.BlockSpec(short_taps.shape, lambda p: (0, 0, 0)),
            pl.BlockSpec(mr_filter.shape, lambda p: (0, 0)),
        ],
        out_specs=[pl.BlockSpec((PACKED, STEP), lambda p: (0, 0))] * slots,
        out_shape=[jax.ShapeDtypeStruct((PACKED, STEP), BF16)] * slots,
        scratch_shapes=[
            pltpu.VMEM((slots, PACKED, STEP), BF16),
            pltpu.VMEM((2, 144, LANES), F32),
            pltpu.VMEM((2, 144, LANES), F32),
        ],
        compiler_params=params(),
        cost_estimate=cost(128 * width * 30, 128 * width * 6),
        name="tail",
    )(queries, keys_in, values_in, keys_in, values_in, short_taps, mr_filter)


def feature_kernel(k_ref, v_ref, taps_ref, out_ref, ks, vs):
    rows = k_ref.shape[0]

    def pair(index, carry):
        for tile in range(2):
            cols = pl.ds(pl.multiple_of(index * 2 * LANES + tile * LANES, LANES), LANES)
            kt, vt = ks.at[tile], vs.at[tile]
            kt[0:8, :] = jnp.zeros((8, LANES), F32)
            vt[0:8, :] = jnp.zeros((8, LANES), F32)
            kt[8 : rows + 8, :] = k_ref[:, cols].astype(F32)
            vt[8 : rows + 8, :] = v_ref[:, cols].astype(F32)
            key_taps = taps_ref[1, :, cols].astype(F32)
            value_taps = taps_ref[2, :, cols].astype(F32)
            for row in range(0, rows, 64):
                key = short_conv(kt, key_taps, row, 64)
                value = short_conv(vt, value_taps, row, 64)
                out_ref[row : row + 64, cols] = (key * value).astype(BF16)
        return carry

    lax.fori_loop(0, k_ref.shape[1] // (2 * LANES), pair, 0)


def feature_call(keys_in, values_in, short_taps):
    rows, width = keys_in.shape
    block = pl.BlockSpec((rows, WIDE), lambda p: (0, p))
    return pl.pallas_call(
        feature_kernel,
        grid=(width // WIDE,),
        in_specs=[block, block, pl.BlockSpec((3, 7, WIDE), lambda p: (0, 0, p))],
        out_specs=block,
        out_shape=jax.ShapeDtypeStruct((rows, width), BF16),
        scratch_shapes=[pltpu.VMEM((2, rows + 8, LANES), F32), pltpu.VMEM((2, rows + 8, LANES), F32)],
        compiler_params=params(),
        cost_estimate=cost(rows * width * 30, rows * width * 6),
        name="features",
    )(keys_in, values_in, short_taps)


def route_kernel(count, pred_ref, *refs):
    ins, outs, (filt_ref, held) = refs[:count], refs[count : 2 * count], refs[2 * count :]
    device = lax.axis_index("seq")
    for slot in range(count):
        held[slot] = ins[slot][...]
    for slot in range(count):
        source = jnp.maximum(pred_ref[jnp.bitwise_xor(device, slot)], 0)
        outs[slot][...] = held[jnp.bitwise_xor(source, device)]
    for j in range(count):
        last = held[jnp.bitwise_xor(device, j), 144:160, :].astype(F32)[8:]
        filt_ref[16 * j : 16 * j + 16, :] = jnp.concatenate([last[:, :LANES], last[:, LANES:]]).astype(BF16)


def route_call(predecessor, received):
    count = len(received)
    piece = jax.ShapeDtypeStruct((PACKED, STEP), BF16)
    results = pl.pallas_call(
        functools.partial(route_kernel, count),
        in_specs=[pl.BlockSpec(memory_space=pltpu.SMEM)] + [pl.BlockSpec(memory_space=pltpu.VMEM)] * count,
        out_specs=[pl.BlockSpec(memory_space=pltpu.VMEM)] * (count + 1),
        out_shape=[piece] * count + [jax.ShapeDtypeStruct((16 * count, LANES), BF16)],
        scratch_shapes=[pltpu.VMEM((count, PACKED, STEP), BF16)],
        compiler_params=params(),
        name="route",
    )(predecessor, *received)
    return results[:count], results[count]


def pick_groups(result, group_size, rows=BLOCK):
    shape = (rows, result.shape[1])
    group = (lax.broadcasted_iota(jnp.int32, shape, 1) & (LANES - 1)) // group_size
    picked = result[:rows]
    for g in range(1, LANES // group_size):
        picked = jnp.where(group == g, result[g * rows : (g + 1) * rows], picked)
    return picked


def main_kernel(group_size, len_ref, q_ref, u_ref, res_ref, taps_ref, filt_ref, mixed_ref, toep_ref, sum_ref, qs, spread, acc):
    step = pl.program_id(0)
    rows = q_ref.shape[0]
    per_lane = LANES // group_size
    length = len_ref[lax.axis_index("seq")]

    @pl.when(step == 0)
    def _():
        tap_count = filt_ref.shape[0]
        tap = lax.broadcasted_iota(jnp.int32, (tap_count, WINDOW), 0)
        place = lax.broadcasted_iota(jnp.int32, (tap_count, WINDOW), 1)
        onehot = (place == WINDOW - BLOCK - tap).astype(BF16)
        spread[...] = lax.dot_general(
            filt_ref[...], onehot, (((0,), (0,)), ((), ())), preferred_element_type=F32
        )
        acc[...] = jnp.zeros_like(acc)

    mixed_ref[0:128, :] = jnp.zeros((128, WIDE), BF16)

    def pair(index, carry):
        for tile in range(2):
            number = index * 2 + tile
            cols = pl.ds(pl.multiple_of(number * LANES, LANES), LANES)
            qt = qs.at[tile]
            qt[0:8, :] = jnp.zeros((8, LANES), F32)
            qt[8 : rows + 8, :] = q_ref[:, cols].astype(F32)
            query_taps = taps_ref[0, :, cols].astype(F32)
            base = pl.multiple_of((step * (WIDE // LANES) + number) * per_lane, per_lane)
            lines = spread[pl.ds(base, per_lane), :]
            blocks = []
            for g in range(per_lane):
                line = jnp.broadcast_to(lines[g : g + 1], (BLOCK, WINDOW))
                blocks.append(pltpu.roll(line, 0, 1, stride=1, stride_axis=0).astype(BF16))
            matrix = jnp.concatenate(blocks)
            toep_ref[pl.ds(pl.multiple_of(number * per_lane * BLOCK, 16), per_lane * BLOCK), :] = matrix
            for start in range(128, rows, 2 * BLOCK):
                windows = []
                for first in (start, start + BLOCK):
                    low = first + BLOCK - WINDOW
                    if low < 0:
                        windows.append(
                            jnp.concatenate([jnp.zeros((-low, LANES), BF16), u_ref[0 : first + BLOCK, cols]])
                        )
                    else:
                        windows.append(u_ref[low : first + BLOCK, cols])
                result = jnp.dot(matrix, jnp.concatenate(windows, axis=1), preferred_element_type=F32)
                picked = pick_groups(result, group_size)
                for half in range(2):
                    first = start + half * BLOCK
                    filtered = picked[:, half * LANES : (half + 1) * LANES]
                    query = short_conv(qt, query_taps, first, BLOCK)
                    row = lax.broadcasted_iota(jnp.int32, (BLOCK, LANES), 0) + first
                    mixed = jnp.where(row < length, query * filtered, 0.0).astype(BF16)
                    mixed_ref[first : first + BLOCK, cols] = mixed
                    summed = res_ref[first : first + BLOCK, cols].astype(F32) + mixed.astype(F32)
                    acc[first - 128 : first - 128 + BLOCK, :] += summed * summed
        return carry

    lax.fori_loop(0, WIDE // (2 * LANES), pair, 0)

    @pl.when(step == pl.num_programs(0) - 1)
    def _():
        sum_ref[...] = jnp.sum(acc[...].T, axis=0, keepdims=True)


def main_call(group_size, stretch_lengths, queries, mixed_in, residual, short_taps, filter_rows):
    rows, width = queries.shape
    per_step = WIDE // group_size
    groups = filter_rows.shape[1]
    block = pl.BlockSpec((rows, WIDE), lambda p, *_: (0, p))
    return pl.pallas_call(
        functools.partial(main_kernel, group_size),
        grid_spec=pltpu.PrefetchScalarGridSpec(
            num_scalar_prefetch=1,
            grid=(width // WIDE,),
            in_specs=[
                block,
                block,
                block,
                pl.BlockSpec((3, 7, WIDE), lambda p, *_: (0, 0, p)),
                pl.BlockSpec(filter_rows.shape, lambda p, *_: (0, 0)),
            ],
            out_specs=[
                block,
                pl.BlockSpec((per_step * BLOCK, WINDOW), lambda p, *_: (p, 0)),
                pl.BlockSpec((1, rows - 128), lambda p, *_: (0, 0)),
            ],
            scratch_shapes=[
                pltpu.VMEM((2, rows + 8, LANES), F32),
                pltpu.VMEM((groups, WINDOW), F32),
                pltpu.VMEM((rows - 128, LANES), F32),
            ],
        ),
        out_shape=[
            jax.ShapeDtypeStruct((rows, width), BF16),
            jax.ShapeDtypeStruct((groups * BLOCK, WINDOW), BF16),
            jax.ShapeDtypeStruct((1, rows - 128), F32),
        ],
        compiler_params=params(),
        cost_estimate=cost(rows * width * 2 * WINDOW * 8, rows * width * 12),
        name="conv",
    )(stretch_lengths, queries, mixed_in, residual, short_taps, filter_rows)


def head_kernel(group_size, slots, swapped, pred_ref, len_ref, *refs):
    prevs, refs = refs[:slots], refs[slots:]
    q_ref, k_ref, v_ref, u_ref, res_ref, taps_ref, toep_ref, kept_ref, mixed_ref, sum_ref, held, qs, ks, vs, acc = refs
    del kept_ref
    step = pl.program_id(0)
    per_lane = LANES // group_size
    device = lax.axis_index("seq")
    length = len_ref[device]
    follows = pred_ref[device] >= 0

    @pl.when(step == 0)
    def _():
        acc[...] = jnp.zeros_like(acc)
        for slot in range(slots):
            held[slot] = prevs[slot][...]

    def pair(index, carry):
        piece = step * (WIDE // STEP) + index
        slot = jnp.bitwise_xor(piece, device) if swapped else piece
        for tile in range(2):
            number = index * 2 + tile
            cols = pl.ds(pl.multiple_of(number * LANES, LANES), LANES)
            here = slice(tile * LANES, (tile + 1) * LANES)
            qt, kt, vt = qs.at[tile], ks.at[tile], vs.at[tile]
            prev = jnp.where(follows, held[slot, 128:PACKED, here].astype(F32), 0.0)
            qt[0:8, :] = prev[0:8]
            kt[0:8, :] = prev[8:16]
            vt[0:8, :] = prev[16:24]
            qt[8 : OPENING + 8, :] = q_ref[:, cols].astype(F32)
            kt[8:24, :] = k_ref[:, cols].astype(F32)
            vt[8:24, :] = v_ref[:, cols].astype(F32)
            query_taps = taps_ref[0, :, cols].astype(F32)
            key = short_conv(kt, taps_ref[1, :, cols].astype(F32), 0, 16)
            value = short_conv(vt, taps_ref[2, :, cols].astype(F32), 0, 16)
            opening = (key * value).astype(BF16)
            state = held[slot, 0:128, here]
            state = jnp.where(follows, state, jnp.zeros_like(state))
            extended = jnp.concatenate([jnp.zeros((64, LANES), BF16), state, opening, u_ref[16:192, cols]])
            windows = jnp.concatenate([extended[0:WINDOW], extended[BLOCK : BLOCK + WINDOW]], axis=1)
            matrix = toep_ref[pl.ds(pl.multiple_of(number * per_lane * BLOCK, 16), per_lane * BLOCK), :]
            result = jnp.dot(matrix, windows, preferred_element_type=F32)
            picked = pick_groups(result, group_size)
            edge = OPENING - 2 * BLOCK
            edge_matrix = jnp.concatenate([matrix[g * BLOCK : g * BLOCK + edge] for g in range(per_lane)])
            edge_result = jnp.dot(edge_matrix, extended[2 * BLOCK : 2 * BLOCK + WINDOW], preferred_element_type=F32)
            parts = [
                (0, BLOCK, picked[:, :LANES]),
                (BLOCK, BLOCK, picked[:, LANES:]),
                (2 * BLOCK, edge, pick_groups(edge_result, group_size, edge)),
            ]
            for first, rows, filtered in parts:
                query = short_conv(qt, query_taps, first, rows)
                row = lax.broadcasted_iota(jnp.int32, (rows, LANES), 0) + first
                mixed = jnp.where(row < length, query * filtered, 0.0).astype(BF16)
                mixed_ref[first : first + rows, cols] = mixed
                summed = res_ref[first : first + rows, cols].astype(F32) + mixed.astype(F32)
                acc[first : first + rows, :] += summed * summed
        return carry

    lax.fori_loop(0, WIDE // STEP, pair, 0)

    @pl.when(step == pl.num_programs(0) - 1)
    def _():
        sum_ref[...] = jnp.sum(acc[...].T, axis=0, keepdims=True)


def head_call(group_size, swapped, predecessor, stretch_lengths, previous, queries, keys_in, values_in, mixed_in, residual, short_taps, toeplitz, mixed):
    rows, width = queries.shape
    slots = len(previous)
    per_step = WIDE // group_size
    block = pl.BlockSpec((OPENING, WIDE), lambda p, *_: (0, p))
    small = pl.BlockSpec((16, WIDE), lambda p, *_: (0, p))
    return pl.pallas_call(
        functools.partial(head_kernel, group_size, slots, swapped),
        grid_spec=pltpu.PrefetchScalarGridSpec(
            num_scalar_prefetch=2,
            grid=(width // WIDE,),
            in_specs=[pl.BlockSpec((PACKED, STEP), lambda p, *_: (0, 0))] * slots
            + [
                block,
                small,
                small,
                pl.BlockSpec((192, WIDE), lambda p, *_: (0, p)),
                block,
                pl.BlockSpec((3, 7, WIDE), lambda p, *_: (0, 0, p)),
                pl.BlockSpec((per_step * BLOCK, WINDOW), lambda p, *_: (p, 0)),
                pl.BlockSpec(memory_space=pl.ANY),
            ],
            out_specs=[block, pl.BlockSpec((1, 256), lambda p, *_: (0, 0))],
            scratch_shapes=[
                pltpu.VMEM((slots, PACKED, STEP), BF16),
                pltpu.VMEM((2, OPENING + 8, LANES), F32),
                pltpu.VMEM((2, 24, LANES), F32),
                pltpu.VMEM((2, 24, LANES), F32),
                pltpu.VMEM((256, LANES), F32),
            ],
        ),
        out_shape=[
            jax.ShapeDtypeStruct((rows, width), BF16),
            jax.ShapeDtypeStruct((1, 256), F32),
        ],
        input_output_aliases={slots + 9: 0},
        compiler_params=params(),
        cost_estimate=cost(128 * width * 2 * WINDOW * 8, 128 * width * 12),
        name="head",
    )(predecessor, stretch_lengths, *previous, queries, keys_in, values_in, mixed_in, residual, short_taps, toeplitz, mixed)


def norm_kernel(channels, first_block, sums, len_ref, *refs):
    sum_refs, (mixed_ref, res_ref, gain_ref), out_ref = refs[:sums], refs[sums : sums + 3], refs[-1]
    rows = mixed_ref.shape[0]
    first = (pl.program_id(0) + first_block) * rows
    length = len_ref[lax.axis_index("seq")]
    total = sum_refs[0][...]
    for ref in sum_refs[1:]:
        total = total + ref[...]
    scale = jnp.broadcast_to(lax.rsqrt(total / channels + EPSILON), (LANES, total.shape[1])).T[:rows]
    valid = lax.broadcasted_iota(jnp.int32, (rows, LANES), 0) + first < length
    for lane in range(0, mixed_ref.shape[1], LANES):
        cols = slice(lane, lane + LANES)
        gain = gain_ref[:, cols].astype(F32)
        summed = res_ref[:, cols].astype(F32) + mixed_ref[:, cols].astype(F32)
        out_ref[:, cols] = jnp.where(valid, summed * scale * gain, 0.0).astype(BF16)


def norm_call(channels, opening, stretch_lengths, totals, mixed, residual, norm_gain, normed=None):
    rows, width = mixed.shape
    size, first_block, steps, lanes = (OPENING, 0, 1, 256) if opening else (128, 1, rows // 128 - 1, 128)
    block = pl.BlockSpec((size, width), lambda p, *_: (p + first_block, 0))
    operands = [*totals, mixed, residual, norm_gain.reshape(1, width)]
    in_specs = [pl.BlockSpec((1, lanes), lambda p, *_: (0, p))] * len(totals)
    in_specs += [block, block, pl.BlockSpec((1, width), lambda p, *_: (0, 0))]
    aliases = {}
    if normed is not None:
        aliases = {len(operands) + 1: 0}
        operands.append(normed)
        in_specs.append(pl.BlockSpec(memory_space=pl.ANY))
    return pl.pallas_call(
        functools.partial(norm_kernel, channels, first_block, len(totals)),
        grid_spec=pltpu.PrefetchScalarGridSpec(
            num_scalar_prefetch=1, grid=(steps,), in_specs=in_specs, out_specs=block
        ),
        out_shape=jax.ShapeDtypeStruct((rows, width), BF16),
        input_output_aliases=aliases,
        compiler_params=params(),
        cost_estimate=cost(steps * size * width * 6, steps * size * width * 6),
        name="norm_opening" if opening else "norm",
    )(stretch_lengths, *operands)


def swap(array, axis, distance):
    size = lax.axis_size(axis)
    return lax.ppermute(array, axis, [(i, i ^ distance) for i in range(size)])


def shares(squares):
    parts = lax.axis_size("mp")
    if parts != 4:
        return [lax.psum(squares, "mp")]
    return [squares] + [swap(squares, "mp", k) for k in range(1, parts)]


def body(queries, keys_in, values_in, residual, short_taps, mr_filter, norm_gain, predecessor, stretch_lengths):
    rows, width = queries.shape
    count = lax.axis_size("seq")
    channels = width * lax.axis_size("mp")
    group_size = width // mr_filter.shape[1]
    two_phase = width // STEP == count == 8 and mr_filter.shape == (16, LANES)
    packed = tail_call(two_phase, two_phase, queries, keys_in, values_in, short_taps, mr_filter)
    if two_phase:
        received = [packed[0]] + [swap(packed[k], "seq", k) for k in range(1, count)]
        mixed_in = feature_call(keys_in, values_in, short_taps)
        routed, filter_rows = route_call(predecessor, received)
        previous = [routed[0]] + [swap(routed[k], "seq", k) for k in range(1, count)]
    else:
        gathered = lax.all_gather(jnp.stack(packed)[None], "seq", axis=0, tiled=True)
        source = jnp.clip(predecessor[lax.axis_index("seq")], 0, count - 1)
        chosen = lax.dynamic_index_in_dim(gathered, source, 0, keepdims=False)
        previous = [chosen[k] for k in range(len(packed))]
        filter_rows = lax.all_gather(mr_filter, "seq", axis=0, tiled=True)
        mixed_in = feature_call(keys_in, values_in, short_taps)
    mixed, toeplitz, squares = main_call(
        group_size, stretch_lengths, queries, mixed_in, residual, short_taps, filter_rows
    )
    normed = norm_call(channels, False, stretch_lengths, shares(squares), mixed, residual, norm_gain)
    mixed, squares = head_call(
        group_size, two_phase, predecessor, stretch_lengths, previous, queries, keys_in, values_in,
        mixed_in, residual, short_taps, toeplitz, mixed,
    )
    normed = norm_call(channels, True, stretch_lengths, shares(squares), mixed, residual, norm_gain, normed)
    return (mixed, normed)


def solution(mesh):
    in_specs = (
        P("seq", "mp"),
        P("seq", "mp"),
        P("seq", "mp"),
        P("seq", "mp"),
        P(None, None, "mp"),
        P("seq", "mp"),
        P("mp"),
        P(),
        P(),
    )
    out_specs = (P("seq", "mp"), P("seq", "mp"))
    return jax.shard_map(body, mesh=mesh, in_specs=in_specs, out_specs=out_specs, check_vma=False)
```

time: 82.1 us -> 78.9 us (0.961)
  blocking collectives: 30.7 us -> 0 us
  starting transfers between devices: 3.54 us -> 29 us
  local copies, waits for them, and re-layouts: 10.9 us -> 2.55 us
  waiting for transfers between devices: 0.01 us -> 6.44 us
  Pallas kernels: 35.1 us -> 38.7 us
    ppermute x0 -> x20, starting transfers between devices: none -> 29 us  [swap(): return lax.ppermute(array, axis, [(i, i ^ distance) for i in range(size)])]
    all_to_all x1 -> x0, blocking collectives: 24.9 us -> none  [exchange(): lax.all_to_all(pieces, 'seq', split_axis=0, concat_axis=0, tiled=True)]
    unnamed x28 -> x52, local copies, waits for them, and re-layouts: 10.9 us -> 1.95 us
    ppermute x0 -> x20, waiting for transfers between devices: none -> 6.44 us  [swap(): return lax.ppermute(array, axis, [(i, i ^ distance) for i in range(size)])]
    psum x1 -> x0, blocking collectives: 5.76 us -> none  [body(): total = lax.psum(squares, 'mp')]
    pallas_call x5 -> x6, Pallas kernels: 24.3 us -> 28 us  [the longest x2 8.04 us: norm_call(): pl.pallas_call(functools.partial(norm_kernel, channels, first_block, len(...]
    all_to_all x1 -> x0, starting transfers between devices: 3.54 us -> none  [exchange(): lax.all_to_all(pieces, 'seq', split_axis=0, concat_axis=0, tiled=True)]
  transfers between devices with their start and end apart: 1 -> 20, of which waited for: 0 -> 5; matrix products, arithmetic and copies ran while one was open for 0% -> 1% of each run, Pallas kernels for 22% -> 29%
where the time goes in v2:
time: 78.9 us; the launch traced here: 77.5 us
  Pallas kernels  38.7 us (49%)
  starting transfers between devices  29 us (37%)
  waiting for transfers between devices  6.44 us (8%)
  local copies, waits for them, and re-layouts  2.55 us (3%)
  between operations  0.82 us (1%)
    ppermute x20, starting transfers between devices, swap(): return lax.ppermute(array, axis, [(i, i ^ distance) for i in range(size)])  29 us
    pallas_call x1, Pallas kernels, main_call(): pl.pallas_call(functools.partial(main_kernel, group_size), grid_spec=pltp...  10.7 us
    pallas_call x2, Pallas kernels, norm_call(): pl.pallas_call(functools.partial(norm_kernel, channels, first_block, len(...  8.04 us
    pallas_call x1, Pallas kernels, head_call(): pl.pallas_call(functools.partial(head_kernel, group_size, slots, swapped)...  7.46 us
    pallas_call x1, Pallas kernels, feature_call(): pl.pallas_call(feature_kernel, grid=(width // WIDE,), in_specs=[block, bl...  6.95 us
    ppermute x20, waiting for transfers between devices, swap(): return lax.ppermute(array, axis, [(i, i ^ distance) for i in range(size)])  6.44 us
    pallas_call x1, Pallas kernels, tail_call(): pl.pallas_call(functools.partial(tail_kernel, slots, swapped, packed), gr...  3.48 us
    pallas_call x1, Pallas kernels, route_call(): pl.pallas_call(functools.partial(route_kernel, count), in_specs=[pl.Block...  2.08 us
  transfers between devices with their start and end apart: 20, of which 5 were waited for; matrix products, arithmetic and copies ran while one was open for 1% of the time, Pallas kernels for 29%

profile of v2, /device:TPU:0, one launch (start us, length us, event | category | flops | bytes accessed | tf_op | source)
XLA Modules:
  0.0 77.5 jit_solution(3654462709839710659)
XLA Ops:
  0.6 3.5 %tail.1 = (bf16[160,256]{1,0:T(8,128)(2,1)}, bf16[160,256]{1,0:T(8,128)(2,1)}, bf16[160,256]{1,0:T(8,128)(2,1)}, bf16[160,256]{1,0:T(8,128)(2,1)}, bf16[160,256]...) custom-call(bf16[512,2048]{1,0:T(8,128)(2,1)} %refs_8_.1, ...), custom_call_target="tpu_custom_call" | custom-call | flops 7864320 | bytes 1572864 | tf_op jit(solution)/shard_map/tail/pallas_call | solution.py:77
  4.1 3.0 %collective-permute-start = (bf16[160,256]{1,0:T(8,128)(2,1)}, bf16[160,256]{1,0:T(8,128)(2,1)S(1)}, u32[]{:S(2)}, u32[]{:S(2)}) collective-permute-start(bf16[160,256]{1,0:T(8,128)(2,1)} %get-tuple-element.25), channel_id=1, source_target_pairs={{0,4},{4,0},{8,12},{12,8},{16,20},{20,16},{24,28},{28,24},{1,5},{5... | collective-permute-start | bytes 245768 | tf_op jit(solution)/shard_map/ppermute | solution.py:433
  7.1 1.6 %collective-permute-start.1 = (bf16[160,256]{1,0:T(8,128)(2,1)}, bf16[160,256]{1,0:T(8,128)(2,1)S(1)}, u32[]{:S(2)}, u32[]{:S(2)}) collective-permute-start(bf16[160,256]{1,0:T(8,128)(2,1)} %get-tuple-element.26), channel_id=1, source_target_pairs={{0,8},{4,12},{8,0},{12,4},{16,24},{20,28},{24,16},{28,20},{1,9},{5... | collective-permute-start | bytes 245768 | tf_op jit(solution)/shard_map/ppermute | solution.py:433
  8.7 3.0 %collective-permute-start.3 = (bf16[160,256]{1,0:T(8,128)(2,1)}, bf16[160,256]{1,0:T(8,128)(2,1)S(1)}, u32[]{:S(2)}, u32[]{:S(2)}) collective-permute-start(bf16[160,256]{1,0:T(8,128)(2,1)} %get-tuple-element.28), channel_id=1, source_target_pairs={{0,16},{4,20},{8,24},{12,28},{16,0},{20,4},{24,8},{28,12},{1,17},{... | collective-permute-start | bytes 245768 | tf_op jit(solution)/shard_map/ppermute | solution.py:433
  11.6 1.3 %collective-permute-start.4 = (bf16[160,256]{1,0:T(8,128)(2,1)}, bf16[160,256]{1,0:T(8,128)(2,1)S(1)}, u32[]{:S(2)}, u32[]{:S(2)}) collective-permute-start(bf16[160,256]{1,0:T(8,128)(2,1)} %get-tuple-element.29), channel_id=1, source_target_pairs={{0,20},{4,16},{8,28},{12,24},{16,4},{20,0},{24,12},{28,8},{1,21},{... | collective-permute-start | bytes 245768 | tf_op jit(solution)/shard_map/ppermute | solution.py:433
  12.9 3.6 %collective-permute-start.5 = (bf16[160,256]{1,0:T(8,128)(2,1)}, bf16[160,256]{1,0:T(8,128)(2,1)S(1)}, u32[]{:S(2)}, u32[]{:S(2)}) collective-permute-start(bf16[160,256]{1,0:T(8,128)(2,1)} %get-tuple-element.30), channel_id=1, source_target_pairs={{0,24},{4,28},{8,16},{12,20},{16,8},{20,12},{24,0},{28,4},{1,25},{... | collective-permute-start | bytes 245768 | tf_op jit(solution)/shard_map/ppermute | solution.py:433
  16.6 7.0 %features.1.u_ref.refs_11_ = bf16[512,2048]{1,0:T(8,128)(2,1)} custom-call(bf16[512,2048]{1,0:T(8,128)(2,1)} %refs_9_.1, bf16[512,2048]{1,0:T(8,128)(2,1)} %refs_10_.1, bf16[3,7,2048]{2,1,0:T(8,128)(2,1)} %refs_13_.1), custom_call_target="tpu_custom_call" | custom-call | flops 31457280 | bytes 6291456 | tf_op jit(solution)/shard_map/features/pallas_call | solution.py:127
  23.6 1.5 %collective-permute-done.4.refs_5_ = bf16[160,256]{1,0:T(8,128)(2,1)S(1)} collective-permute-done((bf16[160,256]{1,0:T(8,128)(2,1)}, bf16[160,256]{1,0:T(8,128)(2,1)S(1)}, u32[]{:S(2)}, u32[]{:S(2)}) %collective-permute-start.4) | collective-permute-done | bytes 81952 | tf_op jit(solution)/shard_map/ppermute | solution.py:433
  25.8 2.1 %route.1 = (bf16[160,256]{1,0:T(8,128)(2,1)}, bf16[160,256]{1,0:T(8,128)(2,1)}, bf16[160,256]{1,0:T(8,128)(2,1)}, bf16[160,256]{1,0:T(8,128)(2,1)}, bf16[160,256...) custom-call(s32[8]{0:T(128)} %pred_ref.3, ...), custom_call_target="tpu_custom_call" | custom-call | tf_op jit(solution)/shard_map/route/pallas_call | solution.py:156
  28.6 3.2 %collective-permute-start.8 = (bf16[160,256]{1,0:T(8,128)(2,1)}, bf16[160,256]{1,0:T(8,128)(2,1)S(1)}, u32[]{:S(2)}, u32[]{:S(2)}) collective-permute-start(bf16[160,256]{1,0:T(8,128)(2,1)} %get-tuple-element.34), channel_id=1, source_target_pairs={{0,8},{4,12},{8,0},{12,4},{16,24},{20,28},{24,16},{28,20},{1,9},{5... | collective-permute-start | bytes 245768 | tf_op jit(solution)/shard_map/ppermute | solution.py:433
  31.7 10.7 %conv.1 = (bf16[512,2048]{1,0:T(8,128)(2,1)}, bf16[8192,256]{1,0:T(8,128)(2,1)}, f32[1,384]{1,0:T(1,128)}) custom-call(s32[8]{0:T(128)} %len_ref.7, bf16[512,2048]{1,0:T(8,128)(2,1)} %refs_8_.1, bf16[512,2048]{1,0:T(8,128)(2,1)} %features.1.u_ref.refs_11_, bf16[512,2048]{1,0:T(8,128)(2,1)} %refs_5_.3, bf16[3,7,2048]{2,1,0:T(8,128)(2,1)} %refs_13_.1, ...), custom_call_target="tpu_custom_call" | custom-call | flops 4294967296 | bytes 12582912 | tf_op jit(solution)/shard_map/conv/pallas_call | solution.py:247
  42.5 1.6 %collective-permute-start.18 = (f32[1,384]{1,0:T(1,128)}, f32[1,384]{1,0:T(1,128)S(1)}, u32[]{:S(2)}, u32[]{:S(2)}) collective-permute-start(f32[1,384]{1,0:T(1,128)} %get-tuple-element.45.refs_0_), channel_id=1, source_target_pairs={{0,2},{1,3},{2,0},{3,1},{4,6},{5,7},{6,4},{7,5},{8,10},{9,11},{10,... | collective-permute-start | bytes 4616 | tf_op jit(solution)/shard_map/ppermute | solution.py:433
  44.3 1.4 %collective-permute-done.19.refs_3_ = f32[1,384]{1,0:T(1,128)S(1)} collective-permute-done((f32[1,384]{1,0:T(1,128)}, f32[1,384]{1,0:T(1,128)S(1)}, u32[]{:S(2)}, u32[]{:S(2)}) %collective-permute-start.19) | collective-permute-done | bytes 1568 | tf_op jit(solution)/shard_map/ppermute | solution.py:433
  45.7 0.8 %collective-permute-start.9 = (bf16[160,256]{1,0:T(8,128)(2,1)S(1)}, bf16[160,256]{1,0:T(8,128)(2,1)S(1)}, u32[]{:S(2)}, u32[]{:S(2)}) collective-permute-start(bf16[160,256]{1,0:T(8,128)(2,1)S(1)} %copy-done.25), channel_id=1, source_target_pairs={{0,12},{4,8},{8,4},{12,0},{16,28},{20,24},{24,20},{28,16},{1,13},{... | collective-permute-start | bytes 245768 | tf_op jit(solution)/shard_map/ppermute | solution.py:433
  46.5 3.2 %collective-permute-start.10 = (bf16[160,256]{1,0:T(8,128)(2,1)S(1)}, bf16[160,256]{1,0:T(8,128)(2,1)S(1)}, u32[]{:S(2)}, u32[]{:S(2)}) collective-permute-start(bf16[160,256]{1,0:T(8,128)(2,1)S(1)} %copy-done.24), channel_id=1, source_target_pairs={{0,16},{4,20},{8,24},{12,28},{16,0},{20,4},{24,8},{28,12},{1,17},{... | collective-permute-start | bytes 245768 | tf_op jit(solution)/shard_map/ppermute | solution.py:433
  50.2 2.9 %collective-permute-start.12 = (bf16[160,256]{1,0:T(8,128)(2,1)S(1)}, bf16[160,256]{1,0:T(8,128)(2,1)S(1)}, u32[]{:S(2)}, u32[]{:S(2)}) collective-permute-start(bf16[160,256]{1,0:T(8,128)(2,1)S(1)} %copy-done.22), channel_id=1, source_target_pairs={{0,24},{4,28},{8,16},{12,20},{16,8},{20,12},{24,0},{28,4},{1,25},{... | collective-permute-start | bytes 245768 | tf_op jit(solution)/shard_map/ppermute | solution.py:433
  53.0 1.6 %collective-permute-start.13 = (bf16[160,256]{1,0:T(8,128)(2,1)S(1)}, bf16[160,256]{1,0:T(8,128)(2,1)S(1)}, u32[]{:S(2)}, u32[]{:S(2)}) collective-permute-start(bf16[160,256]{1,0:T(8,128)(2,1)S(1)} %copy-done.21), channel_id=1, source_target_pairs={{0,28},{4,24},{8,20},{12,16},{16,12},{20,8},{24,4},{28,0},{1,29},{... | collective-permute-start | bytes 245768 | tf_op jit(solution)/shard_map/ppermute | solution.py:433
  55.3 5.0 %norm.1.refs_7_ = bf16[512,2048]{1,0:T(8,128)(2,1)} custom-call(s32[8]{0:T(128)} %len_ref.7, f32[1,384]{1,0:T(1,128)} %get-tuple-element.45.refs_0_, f32[1,384]{1,0:T(1,128)} %copy-done.17, f32[1,384]{1,0:T(1,128)} %copy-done.16, f32[1,384]{1,0:T(1,128)} %copy-done.15, bf16[512,2048]{1,0:T(8,128)(2,1)} %get-tuple-element.42.refs_15_.refs_4_, ...), custom_call_target="tpu_custom_call" | custom-call | flops 4718592 | bytes 4718592 | tf_op jit(solution)/shard_map/norm/pallas_call | solution.py:418
  60.3 1.7 %collective-permute-done.11.refs_5_ = bf16[160,256]{1,0:T(8,128)(2,1)S(1)} collective-permute-done((bf16[160,256]{1,0:T(8,128)(2,1)S(1)}, bf16[160,256]{1,0:T(8,128)(2,1)S(1)}, u32[]{:S(2)}, u32[]{:S(2)}) %collective-permute-start.11) | collective-permute-done | bytes 81952 | tf_op jit(solution)/shard_map/ppermute | solution.py:433
  62.7 7.5 %head.1 = (bf16[512,2048]{1,0:T(8,128)(2,1)}, f32[1,256]{1,0:T(1,128)}) custom-call(s32[8]{0:T(128)} %pred_ref.3, s32[8]{0:T(128)} %len_ref.7, bf16[160,256]{1,0:T(8,128)(2,1)} %get-tuple-element.32.refs_0_, bf16[160,256]{1,0:T(8,128)(2,1)} %copy-done.7, bf16[160,256]{1,0:T(8,128)(2,1)} %copy-done.8, ...), custom_call_target="tpu_custom_call", output_to_operand_aliasing={{0}: (17, {})} | custom-call | flops 1073741824 | bytes 3145728 | tf_op jit(solution)/shard_map/head/pallas_call | solution.py:353
  70.2 0.8 %collective-permute-start.15 = (f32[1,256]{1,0:T(1,128)}, f32[1,256]{1,0:T(1,128)S(1)}, u32[]{:S(2)}, u32[]{:S(2)}) collective-permute-start(f32[1,256]{1,0:T(1,128)} %get-tuple-element.44.refs_0_), channel_id=1, source_target_pairs={{0,2},{1,3},{2,0},{3,1},{4,6},{5,7},{6,4},{7,5},{8,10},{9,11},{10,... | collective-permute-start | bytes 3080 | tf_op jit(solution)/shard_map/ppermute | solution.py:433
  71.0 1.1 %collective-permute-start.14 = (f32[1,256]{1,0:T(1,128)}, f32[1,256]{1,0:T(1,128)S(1)}, u32[]{:S(2)}, u32[]{:S(2)}) collective-permute-start(f32[1,256]{1,0:T(1,128)} %get-tuple-element.44.refs_0_), channel_id=1, source_target_pairs={{0,1},{1,0},{2,3},{3,2},{4,5},{5,4},{6,7},{7,6},{8,9},{9,8},{10,11... | collective-permute-start | bytes 3080 | tf_op jit(solution)/shard_map/ppermute | solution.py:433
  72.1 1.3 %collective-permute-done.16.refs_3_ = f32[1,256]{1,0:T(1,128)S(1)} collective-permute-done((f32[1,256]{1,0:T(1,128)}, f32[1,256]{1,0:T(1,128)S(1)}, u32[]{:S(2)}, u32[]{:S(2)}) %collective-permute-start.16) | collective-permute-done | bytes 1056 | tf_op jit(solution)/shard_map/ppermute | solution.py:433
  74.5 3.0 %norm_opening.1 = bf16[512,2048]{1,0:T(8,128)(2,1)} custom-call(s32[8]{0:T(128)} %len_ref.7, f32[1,256]{1,0:T(1,128)} %get-tuple-element.44.refs_0_, f32[1,256]{1,0:T(1,128)} %copy-done.20, f32[1,256]{1,0:T(1,128)} %copy-done.19, f32[1,256]{1,0:T(1,128)} %copy-done.18, bf16[512,2048]{1,0:T(8,128)(2,1)} %get-tuple-element.22.refs_4_, ...), custom_call_target="tpu_custom_call", output_to_operand_aliasing={{}: (8, {})} | custom-call | flops 1769472 | bytes 1769472 | tf_op jit(solution)/shard_map/norm_opening/pallas_call | solution.py:418
  (76 shorter events, 4.6 us)
Async XLA Ops:
  4.1 8.8 %collective-permute-start = (bf16[160,256]{1,0:T(8,128)(2,1)}, bf16[160,256]{1,0:T(8,128)(2,1)S(1)}, u32[]{:S(2)}, u32[]{:S(2)}) collective-permute-start(bf16[160,256]{1,0:T(8,128)(2,1)} %get-tuple-element.25), channel_id=1, source_target_pairs={{0,4},{4,0},{8,12},{12,8},{16,20},{20,16},{24,28},{28,24},{1,5},{5... | collective-permute-start | bytes 245768 | tf_op jit(solution)/shard_map/ppermute | solution.py:433
  7.1 9.5 %collective-permute-start.1 = (bf16[160,256]{1,0:T(8,128)(2,1)}, bf16[160,256]{1,0:T(8,128)(2,1)S(1)}, u32[]{:S(2)}, u32[]{:S(2)}) collective-permute-start(bf16[160,256]{1,0:T(8,128)(2,1)} %get-tuple-element.26), channel_id=1, source_target_pairs={{0,8},{4,12},{8,0},{12,4},{16,24},{20,28},{24,16},{28,20},{1,9},{5... | collective-permute-start | bytes 245768 | tf_op jit(solution)/shard_map/ppermute | solution.py:433
  8.7 14.9 %collective-permute-start.2 = (bf16[160,256]{1,0:T(8,128)(2,1)}, bf16[160,256]{1,0:T(8,128)(2,1)S(1)}, u32[]{:S(2)}, u32[]{:S(2)}) collective-permute-start(bf16[160,256]{1,0:T(8,128)(2,1)} %get-tuple-element.27), channel_id=1, source_target_pairs={{0,12},{4,8},{8,4},{12,0},{16,28},{20,24},{24,20},{28,16},{1,13},{... | collective-permute-start | bytes 245768 | tf_op jit(solution)/shard_map/ppermute | solution.py:433
  8.7 14.9 %collective-permute-start.3 = (bf16[160,256]{1,0:T(8,128)(2,1)}, bf16[160,256]{1,0:T(8,128)(2,1)S(1)}, u32[]{:S(2)}, u32[]{:S(2)}) collective-permute-start(bf16[160,256]{1,0:T(8,128)(2,1)} %get-tuple-element.28), channel_id=1, source_target_pairs={{0,16},{4,20},{8,24},{12,28},{16,0},{20,4},{24,8},{28,12},{1,17},{... | collective-permute-start | bytes 245768 | tf_op jit(solution)/shard_map/ppermute | solution.py:433
  11.6 13.4 %collective-permute-start.4 = (bf16[160,256]{1,0:T(8,128)(2,1)}, bf16[160,256]{1,0:T(8,128)(2,1)S(1)}, u32[]{:S(2)}, u32[]{:S(2)}) collective-permute-start(bf16[160,256]{1,0:T(8,128)(2,1)} %get-tuple-element.29), channel_id=1, source_target_pairs={{0,20},{4,16},{8,28},{12,24},{16,4},{20,0},{24,12},{28,8},{1,21},{... | collective-permute-start | bytes 245768 | tf_op jit(solution)/shard_map/ppermute | solution.py:433
  12.9 12.2 %collective-permute-start.5 = (bf16[160,256]{1,0:T(8,128)(2,1)}, bf16[160,256]{1,0:T(8,128)(2,1)S(1)}, u32[]{:S(2)}, u32[]{:S(2)}) collective-permute-start(bf16[160,256]{1,0:T(8,128)(2,1)} %get-tuple-element.30), channel_id=1, source_target_pairs={{0,24},{4,28},{8,16},{12,20},{16,8},{20,12},{24,0},{28,4},{1,25},{... | collective-permute-start | bytes 245768 | tf_op jit(solution)/shard_map/ppermute | solution.py:433
  16.5 8.6 %collective-permute-start.6 = (bf16[160,256]{1,0:T(8,128)(2,1)}, bf16[160,256]{1,0:T(8,128)(2,1)S(1)}, u32[]{:S(2)}, u32[]{:S(2)}) collective-permute-start(bf16[160,256]{1,0:T(8,128)(2,1)} %get-tuple-element.31), channel_id=1, source_target_pairs={{0,28},{4,24},{8,20},{12,16},{16,12},{20,8},{24,4},{28,0},{1,29},{... | collective-permute-start | bytes 245768 | tf_op jit(solution)/shard_map/ppermute | solution.py:433
  27.9 22.3 %collective-permute-start.7 = (bf16[160,256]{1,0:T(8,128)(2,1)}, bf16[160,256]{1,0:T(8,128)(2,1)S(1)}, u32[]{:S(2)}, u32[]{:S(2)}) collective-permute-start(bf16[160,256]{1,0:T(8,128)(2,1)} %get-tuple-element.33), channel_id=1, source_target_pairs={{0,4},{4,0},{8,12},{12,8},{16,20},{20,16},{24,28},{28,24},{1,5},{5... | collective-permute-start | bytes 245768 | tf_op jit(solution)/shard_map/ppermute | solution.py:433
  28.6 24.5 %collective-permute-start.8 = (bf16[160,256]{1,0:T(8,128)(2,1)}, bf16[160,256]{1,0:T(8,128)(2,1)S(1)}, u32[]{:S(2)}, u32[]{:S(2)}) collective-permute-start(bf16[160,256]{1,0:T(8,128)(2,1)} %get-tuple-element.34), channel_id=1, source_target_pairs={{0,8},{4,12},{8,0},{12,4},{16,24},{20,28},{24,16},{28,20},{1,9},{5... | collective-permute-start | bytes 245768 | tf_op jit(solution)/shard_map/ppermute | solution.py:433
  31.7 18.0 %copy-start.23 = (bf16[160,256]{1,0:T(8,128)(2,1)S(1)}, bf16[160,256]{1,0:T(8,128)(2,1)}, u32[]{:S(2)}) copy-start(bf16[160,256]{1,0:T(8,128)(2,1)} %get-tuple-element.37) | copy-start | bytes 245764
  31.7 18.4 %copy-start.22 = (bf16[160,256]{1,0:T(8,128)(2,1)S(1)}, bf16[160,256]{1,0:T(8,128)(2,1)}, u32[]{:S(2)}) copy-start(bf16[160,256]{1,0:T(8,128)(2,1)} %get-tuple-element.38) | copy-start | bytes 245764
  31.7 21.3 %copy-start.21 = (bf16[160,256]{1,0:T(8,128)(2,1)S(1)}, bf16[160,256]{1,0:T(8,128)(2,1)}, u32[]{:S(2)}) copy-start(bf16[160,256]{1,0:T(8,128)(2,1)} %get-tuple-element.39) | copy-start | bytes 245764
  31.7 22.9 %copy-start.14 = (bf16[2048]{0:T(1024)(128)(2,1)S(1)}, bf16[2048]{0:T(1024)(128)(2,1)}, u32[]{:S(2)}) copy-start(bf16[2048]{0:T(1024)(128)(2,1)} %param.15) | copy-start | bytes 12292
  42.4 3.2 %collective-permute-start.19 = (f32[1,384]{1,0:T(1,128)}, f32[1,384]{1,0:T(1,128)S(1)}, u32[]{:S(2)}, u32[]{:S(2)}) collective-permute-start(f32[1,384]{1,0:T(1,128)} %get-tuple-element.45.refs_0_), channel_id=1, source_target_pairs={{0,3},{1,2},{2,1},{3,0},{4,7},{5,6},{6,5},{7,4},{8,11},{9,10},{10,... | collective-permute-start | bytes 4616 | tf_op jit(solution)/shard_map/ppermute | solution.py:433
  42.5 4.0 %collective-permute-start.18 = (f32[1,384]{1,0:T(1,128)}, f32[1,384]{1,0:T(1,128)S(1)}, u32[]{:S(2)}, u32[]{:S(2)}) collective-permute-start(f32[1,384]{1,0:T(1,128)} %get-tuple-element.45.refs_0_), channel_id=1, source_target_pairs={{0,2},{1,3},{2,0},{3,1},{4,6},{5,7},{6,4},{7,5},{8,10},{9,11},{10,... | collective-permute-start | bytes 4616 | tf_op jit(solution)/shard_map/ppermute | solution.py:433
  44.0 5.7 %collective-permute-start.17 = (f32[1,384]{1,0:T(1,128)}, f32[1,384]{1,0:T(1,128)S(1)}, u32[]{:S(2)}, u32[]{:S(2)}) collective-permute-start(f32[1,384]{1,0:T(1,128)} %get-tuple-element.45.refs_0_), channel_id=1, source_target_pairs={{0,1},{1,0},{2,3},{3,2},{4,5},{5,4},{6,7},{7,6},{8,9},{9,8},{10,11... | collective-permute-start | bytes 4616 | tf_op jit(solution)/shard_map/ppermute | solution.py:433
  45.7 14.6 %collective-permute-start.9 = (bf16[160,256]{1,0:T(8,128)(2,1)S(1)}, bf16[160,256]{1,0:T(8,128)(2,1)S(1)}, u32[]{:S(2)}, u32[]{:S(2)}) collective-permute-start(bf16[160,256]{1,0:T(8,128)(2,1)S(1)} %copy-done.25), channel_id=1, source_target_pairs={{0,12},{4,8},{8,4},{12,0},{16,28},{20,24},{24,20},{28,16},{1,13},{... | collective-permute-start | bytes 245768 | tf_op jit(solution)/shard_map/ppermute | solution.py:433
  46.5 13.8 %collective-permute-start.10 = (bf16[160,256]{1,0:T(8,128)(2,1)S(1)}, bf16[160,256]{1,0:T(8,128)(2,1)S(1)}, u32[]{:S(2)}, u32[]{:S(2)}) collective-permute-start(bf16[160,256]{1,0:T(8,128)(2,1)S(1)} %copy-done.24), channel_id=1, source_target_pairs={{0,16},{4,20},{8,24},{12,28},{16,0},{20,4},{24,8},{28,12},{1,17},{... | collective-permute-start | bytes 245768 | tf_op jit(solution)/shard_map/ppermute | solution.py:433
  49.7 12.3 %collective-permute-start.11 = (bf16[160,256]{1,0:T(8,128)(2,1)S(1)}, bf16[160,256]{1,0:T(8,128)(2,1)S(1)}, u32[]{:S(2)}, u32[]{:S(2)}) collective-permute-start(bf16[160,256]{1,0:T(8,128)(2,1)S(1)} %copy-done.23), channel_id=1, source_target_pairs={{0,20},{4,16},{8,28},{12,24},{16,4},{20,0},{24,12},{28,8},{1,21},{... | collective-permute-start | bytes 245768 | tf_op jit(solution)/shard_map/ppermute | solution.py:433
  50.2 11.9 %collective-permute-start.12 = (bf16[160,256]{1,0:T(8,128)(2,1)S(1)}, bf16[160,256]{1,0:T(8,128)(2,1)S(1)}, u32[]{:S(2)}, u32[]{:S(2)}) collective-permute-start(bf16[160,256]{1,0:T(8,128)(2,1)S(1)} %copy-done.22), channel_id=1, source_target_pairs={{0,24},{4,28},{8,16},{12,20},{16,8},{20,12},{24,0},{28,4},{1,25},{... | collective-permute-start | bytes 245768 | tf_op jit(solution)/shard_map/ppermute | solution.py:433
  53.0 9.0 %collective-permute-start.13 = (bf16[160,256]{1,0:T(8,128)(2,1)S(1)}, bf16[160,256]{1,0:T(8,128)(2,1)S(1)}, u32[]{:S(2)}, u32[]{:S(2)}) collective-permute-start(bf16[160,256]{1,0:T(8,128)(2,1)S(1)} %copy-done.21), channel_id=1, source_target_pairs={{0,28},{4,24},{8,20},{12,16},{16,12},{20,8},{24,4},{28,0},{1,29},{... | collective-permute-start | bytes 245768 | tf_op jit(solution)/shard_map/ppermute | solution.py:433
  70.2 3.3 %collective-permute-start.16 = (f32[1,256]{1,0:T(1,128)}, f32[1,256]{1,0:T(1,128)S(1)}, u32[]{:S(2)}, u32[]{:S(2)}) collective-permute-start(f32[1,256]{1,0:T(1,128)} %get-tuple-element.44.refs_0_), channel_id=1, source_target_pairs={{0,3},{1,2},{2,1},{3,0},{4,7},{5,6},{6,5},{7,4},{8,11},{9,10},{10,... | collective-permute-start | bytes 3080 | tf_op jit(solution)/shard_map/ppermute | solution.py:433
  70.2 3.7 %collective-permute-start.15 = (f32[1,256]{1,0:T(1,128)}, f32[1,256]{1,0:T(1,128)S(1)}, u32[]{:S(2)}, u32[]{:S(2)}) collective-permute-start(f32[1,256]{1,0:T(1,128)} %get-tuple-element.44.refs_0_), channel_id=1, source_target_pairs={{0,2},{1,3},{2,0},{3,1},{4,6},{5,7},{6,4},{7,5},{8,10},{9,11},{10,... | collective-permute-start | bytes 3080 | tf_op jit(solution)/shard_map/ppermute | solution.py:433
  71.0 2.9 %collective-permute-start.14 = (f32[1,256]{1,0:T(1,128)}, f32[1,256]{1,0:T(1,128)S(1)}, u32[]{:S(2)}, u32[]{:S(2)}) collective-permute-start(f32[1,256]{1,0:T(1,128)} %get-tuple-element.44.refs_0_), channel_id=1, source_target_pairs={{0,1},{1,0},{2,3},{3,2},{4,5},{5,4},{6,7},{7,6},{8,9},{9,8},{10,11... | collective-permute-start | bytes 3080 | tf_op jit(solution)/shard_map/ppermute | solution.py:433
  (22 other events, 99.9 us)
